TPU v7x, 32 devices: a whole 2x2x4 slice. The times are simulated.
32 devices in a mesh: px: 4 (over x, core), py: 8 (over z, y).
Axes of the slice: x: 2, y: 2, z: 4, core: 2. Of those that a mesh axis runs over, the one named last changes fastest.
Arguments:
- right_side: float32 [4, 8, 16, 8, 128], P('px', 'py'), may hold values from -6 to 6
- live_blocks: int32 [4, 8], P('px', 'py'), may hold values from 8 to 16, as said below
- diag_fine: float32 [4, 8, 16, 128, 128], P('px', 'py')
- couple_fine: float32 [4, 8, 16, 4, 128, 128], P('px', 'py'), may hold values from -0.125 to 0.125
- links_fine: int32 [4, 8, 16, 4], P('px', 'py'), may hold values from 0 to 31
- send_fine: int32 [4, 8, 4], P('px', 'py'), may hold values from 0 to 7
- prolong_fine: float32 [4, 8, 16, 128, 128], P('px', 'py'), may hold values from -0.25 to 0.25
- owner_fine: int32 [4, 8, 16], P('px', 'py'), may hold values from 0 to 3
- diag_mid: float32 [4, 8, 4, 128, 128], P('px', 'py')
- couple_mid: float32 [4, 8, 4, 4, 128, 128], P('px', 'py'), may hold values from -0.125 to 0.125
- links_mid: int32 [4, 8, 4, 4], P('px', 'py'), may hold values from 0 to 7
- send_mid: int32 [4, 8, 1], P('px', 'py'), may hold values from 0 to 3
- prolong_mid: float32 [4, 8, 4, 128, 128], P('px', 'py'), may hold values from -0.375 to 0.375
- owner_mid: int32 [4, 8, 4], P('px', 'py'), may hold values from 0 to 3
- diag_row: float32 [4, 4, 128, 128], P('px')
- couple_row: float32 [4, 4, 4, 128, 128], P('px'), may hold values from -0.125 to 0.125
- links_row: int32 [4, 4, 4], P('px'), may hold values from 0 to 5
- send_row: int32 [4, 1], P('px'), may hold values from 0 to 3
- prolong_row: float32 [4, 4, 128, 128], P('px'), may hold values from -0.375 to 0.375
- owner_row: int32 [4, 4], P('px'), may hold values from 0 to 3
- coarse_inverse: float32 [512, 512], replicated, may hold values from -0.25 to 0.25
- cheb_low: float32 [3], replicated, may hold values from 0.3 to 0.8
- cheb_high: float32 [3], replicated, may hold values from 6.5 to 9
Outputs:
- solution: float32 [4, 8, 16, 8, 128], P('px', 'py')
- residual: float32 [4, 8, 16, 8, 128], P('px', 'py')
Inputs may be any that keep to these rules, and one draw needn't show every extreme that they name: `live_blocks`: each partition's live fine blocks are its first ones, the rest of its 16 blocks are padding.
All inputs are finite; a program needn't handle non-finite values.
Results may differ from a plain program's by a relative error of at most 0.000092.
Values sent between devices are 32-bit elements; how exact they have to be, the bound alone decides.
A program may use at most 64 MiB of HBM per device.

v0:
```python
import jax
import jax.numpy as jnp
from jax import lax
from jax.sharding import PartitionSpec as P

HIGHEST = lax.Precision.HIGHEST


def padded_2(x, sides, width):
    for axis, dim in sides:
        count, length = (lax.axis_size(axis), x.shape[dim])
        up = [(i, (i + 1) % count) for i in range(count - 1)]
        down = [(j, i) for i, j in up]
        last = lax.slice_in_dim(x, length - width, length, axis=dim)
        initial = lax.slice_in_dim(x, 0, width, axis=dim)
        before = lax.ppermute(last, axis, up)
        after = lax.ppermute(initial, axis, down)
        x = jnp.concatenate([before, x, after], axis=dim)
    return x


def chebyshev_terms(low_bound, high_bound):
    center_value = 0.5 * (high_bound + low_bound)
    half_width = 0.5 * (high_bound - low_bound)
    sigma_ratio = center_value / half_width
    first_rho = 1.0 / sigma_ratio
    second_rho = 1.0 / (2.0 * sigma_ratio - first_rho)
    return (center_value, second_rho * first_rho, 2.0 * second_rho / half_width)


def smooth(apply_fn, target, initial, cheb_terms, keep_last):
    center_value, carry_coef, gain_coef = cheb_terms
    if initial is None:
        residue = target
    else:
        residue = target - apply_fn(initial)
    update = residue / center_value
    if initial is None:
        solution = update
    else:
        solution = initial + update
    residue = residue - apply_fn(update)
    update = carry_coef * update + gain_coef * residue
    solution = solution + update
    if keep_last:
        residue = residue - apply_fn(update)
    return (solution, residue)


def block_apply(vector, diagonal, coupling, link_ids, send_ids, faces_fn):
    lead_dims = link_ids.ndim - 2
    sent_blocks = jnp.take_along_axis(vector, send_ids[..., None, None], axis=lead_dims)
    padded = faces_fn(sent_blocks)
    if lead_dims == 2:
        neighbours = [padded[:-2, 1:-1], padded[2:, 1:-1], padded[1:-1, :-2], padded[1:-1, 2:]]
    else:
        neighbours = [padded[:-2], padded[2:]]
    extended = jnp.concatenate([vector] + neighbours, axis=lead_dims)
    flat_links = link_ids.reshape(link_ids.shape[:lead_dims] + (-1,))
    picked = jnp.take_along_axis(extended, flat_links[..., None, None], axis=lead_dims)
    picked = picked.reshape(link_ids.shape + vector.shape[-2:])
    own_part = jnp.einsum("...brn,...bnm->...brm", vector, diagonal, precision=HIGHEST)
    far_part = jnp.einsum("...bkrn,...bknm->...brm", picked, coupling, precision=HIGHEST)
    return own_part + far_part


def restrict(residue, prolong, owners, block_count):
    pieces = jnp.einsum("...brf,...bcf->...brc", residue, prolong, precision=HIGHEST)
    one_hot = (owners[..., None] == jnp.arange(block_count, dtype=jnp.int32)).astype(jnp.float32)
    return jnp.einsum("...bc,...brn->...crn", one_hot, pieces, precision=HIGHEST)


def prolong_add(coarse, prolong, owners, block_count):
    one_hot = (owners[..., None] == jnp.arange(block_count, dtype=jnp.int32)).astype(jnp.float32)
    picked = jnp.einsum("...bc,...crn->...brn", one_hot, coarse, precision=HIGHEST)
    return jnp.einsum("...brc,...bcf->...brf", picked, prolong, precision=HIGHEST)


def coarse_solve(residue, inverse):
    num_blocks, num_sides, num_nodes = residue.shape
    flattened = jnp.transpose(residue, (1, 0, 2)).reshape(num_sides, num_blocks * num_nodes)
    solved = jnp.dot(flattened, inverse, precision=HIGHEST)
    return jnp.transpose(solved.reshape(num_sides, num_blocks, num_nodes), (1, 0, 2))


def grid_faces(sent_blocks):
    return padded_2(sent_blocks, (("px", 0), ("py", 1)), 1)


def row_faces(sent_blocks):
    return padded_2(sent_blocks, (("px", 0),), 1)


def body(
    right_side,
    live_blocks,
    diag_fine,
    couple_fine,
    links_fine,
    send_fine,
    prolong_fine,
    owner_fine,
    diag_mid,
    couple_mid,
    links_mid,
    send_mid,
    prolong_mid,
    owner_mid,
    diag_row,
    couple_row,
    links_row,
    send_row,
    prolong_row,
    owner_row,
    coarse_inverse,
    cheb_low,
    cheb_high,
):
    fine_count = diag_fine.shape[2]
    mid_count = diag_mid.shape[2]
    row_count = diag_row.shape[1]
    top_count = coarse_inverse.shape[0] // diag_row.shape[-1]
    live_mask = (
        jnp.arange(fine_count, dtype=jnp.int32)[None, None, :] < live_blocks[:, :, None]
    ).astype(jnp.float32)[..., None, None]
    cheb_terms = [
        chebyshev_terms(cheb_low[level_index], cheb_high[level_index]) for level_index in range(3)
    ]

    def apply_fine(vector):
        return (
            block_apply(vector, diag_fine, couple_fine, links_fine, send_fine, grid_faces)
            * live_mask
        )

    def apply_mid(vector):
        return block_apply(vector, diag_mid, couple_mid, links_mid, send_mid, grid_faces)

    def apply_row(vector):
        return block_apply(vector, diag_row, couple_row, links_row, send_row, row_faces)

    fine_target = right_side * live_mask
    fine_sol, fine_res = smooth(apply_fine, fine_target, None, cheb_terms[0], True)
    mid_target = restrict(fine_res, prolong_fine, owner_fine, mid_count)
    mid_sol, mid_res = smooth(apply_mid, mid_target, None, cheb_terms[1], True)
    row_share = restrict(mid_res, prolong_mid, owner_mid, row_count)
    row_target = lax.psum(row_share[:, 0], "py")
    row_sol, row_res = smooth(apply_row, row_target, None, cheb_terms[2], True)
    top_part = jnp.sum(restrict(row_res, prolong_row, owner_row, top_count), axis=0)
    top_target = lax.psum(top_part, "px")
    top_sol = coarse_solve(top_target, coarse_inverse)
    spread_top = top_sol[None]
    row_sol = row_sol + prolong_add(spread_top, prolong_row, owner_row, top_count)
    row_sol, unused_row = smooth(apply_row, row_target, row_sol, cheb_terms[2], False)
    lifted = row_sol[:, None]
    mid_sol = mid_sol + prolong_add(lifted, prolong_mid, owner_mid, row_count)
    mid_sol, unused_mid = smooth(apply_mid, mid_target, mid_sol, cheb_terms[1], False)
    fine_sol = fine_sol + prolong_add(mid_sol, prolong_fine, owner_fine, mid_count) * live_mask
    fine_sol, fine_res = smooth(apply_fine, fine_target, fine_sol, cheb_terms[0], True)
    return (fine_sol, fine_res)


def solution(mesh):
    return jax.shard_map(
        body,
        mesh=mesh,
        in_specs=(
            P("px", "py", None, None, None),
            P("px", "py"),
            P("px", "py", None, None, None),
            P("px", "py", None, None, None, None),
            P("px", "py", None, None),
            P("px", "py", None),
            P("px", "py", None, None, None),
            P("px", "py", None),
            P("px", "py", None, None, None),
            P("px", "py", None, None, None, None),
            P("px", "py", None, None),
            P("px", "py", None),
            P("px", "py", None, None, None),
            P("px", "py", None),
            P("px", None, None, None),
            P("px", None, None, None, None),
            P("px", None, None),
            P("px", None),
            P("px", None, None, None),
            P("px", None),
            P(),
            P(),
            P(),
        ),
        out_specs=(P("px", "py", None, None, None), P("px", "py", None, None, None)),
        check_vma=False,
    )
```

profile of v0, /device:TPU:18, one launch (start us, length us, event | category | flops | bytes accessed | tf_op | source)
XLA Modules:
  0.0 332.8 jit_solution(17298066277295641228)
XLA Ops:
  9.0 2.4 collective-permute-start
  17.0 3.3 collective-permute-start.3
  20.3 2.5 collective-permute-start.2
  22.9 4.3 %collective-permute-done.2 = f32[3,1,4,8,128]{4,3,2,1,0:T(8,128)S(1)} collective-permute-done((f32[3,1,4,8,128]{4,3,2,1,0:T(8,128)S(1)}, f32[3,1,4,8,128]{4,3,2,1,0:T(8,128)S(1)}, u32[]{:S(2)}, u32[]{:S(2)}) %collective-permute-start.2) | collective-permute-done | bytes 49184 | tf_op jit(solution)/shard_map/ppermute | solution.py:16
  28.0 3.8 %fusion.28 = f32[16,8,128]{2,1,0:T(8,128)S(1)} fusion(f32[16,4,8,128]{3,2,1,0:T(8,128)S(1)} %bitcast.468, f32[1,1,16,4,128,128]{5,4,3,2,1,0:T(8,128)} %param.38), kind=kOutput, calls=%fused_computation.52 | convolution fusion | flops 100663296 | bytes 4521984 | tf_op jit(solution)/shard_map/...bkrn,...bknm->...brm/dot_general | solution.py:63
  33.6 2.4 collective-permute-start.5
  43.0 3.9 %collective-permute-start.6 = (f32[3,1,4,8,128]{4,3,2,1,0:T(8,128)S(1)}, f32[3,1,4,8,128]{4,3,2,1,0:T(8,128)S(1)}, u32[]{:S(2)}, u32[]{:S(2)}) collective-permute-start(f32[3,1,4,8,128]{4,3,2,1,0:T(8,128)S(1)} %pad_maximum_fusion.1), channel_id=1, source_target_pairs={{0,1},{1,2},{2,3},{3,4},{4,5},{5,6},{6,7},{8,9},{9,10},{10,11},{11... | collective-permute-start | bytes 147464 | tf_op jit(solution)/shard_map/ppermute | solution.py:16
  46.9 2.9 collective-permute-done.6
  50.7 3.9 %fusion.31 = f32[16,8,128]{2,1,0:T(8,128)S(1)} fusion(f32[16,4,8,128]{3,2,1,0:T(8,128)S(1)} %bitcast.469, f32[1,1,16,4,128,128]{5,4,3,2,1,0:T(8,128)} %param.38), kind=kOutput, calls=%fused_computation.53 | convolution fusion | flops 100663296 | bytes 4521984 | tf_op jit(solution)/shard_map/...bkrn,...bknm->...brm/dot_general | solution.py:63
  55.7 3.1 fusion.70
  60.8 2.3 collective-permute-start.9
  63.0 2.6 collective-permute-start.8
  69.1 2.9 collective-permute-start.11
  72.1 2.9 collective-permute-start.10
  89.4 3.0 collective-permute-start.12
  97.1 2.6 copy.126
  100.4 2.7 collective-permute-start.15
  103.1 3.1 collective-permute-start.14
  120.3 30.6 %psum.14 = f32[1,4,8,128]{3,2,1,0:T(8,128)S(1)} all-reduce(f32[1,4,8,128]{3,2,1,0:T(8,128)} %bitcast.499), channel_id=1, replica_groups=mesh['px'=4,'py'=8] {'py'}, use_global_device_ids=true, to_apply=%region_0.5 | all-reduce | flops 4096 | bytes 32768 | tf_op jit(solution)/shard_map/psum | solution.py:147
  152.8 2.4 collective-permute-start.16
  165.2 2.6 collective-permute-start.18
  178.0 11.3 %psum.15 = f32[8,512]{1,0:T(8,128)} all-reduce(f32[8,512]{1,0:T(8,128)} %bitcast.500), channel_id=1, replica_groups=mesh['px'=4,'py'=8] {'px'}, use_global_device_ids=true, to_apply=%region_1.8 | all-reduce | flops 4096 | bytes 32768 | tf_op jit(solution)/shard_map/psum | solution.py:150
  195.6 2.4 collective-permute-start.20
  207.5 2.4 collective-permute-start.22
  220.1 2.4 collective-permute-start.24
  222.5 2.5 collective-permute-done.24
  225.0 2.5 collective-permute-start.27
  227.6 3.3 collective-permute-start.26
  232.2 3.1 collective-permute-done.26
  240.1 2.4 collective-permute-start.28
  242.5 2.5 collective-permute-done.28
  245.0 3.9 %collective-permute-start.31 = (f32[3,1,1,8,128]{4,2,3,1,0:T(1,128)S(1)}, f32[3,1,1,8,128]{4,2,3,1,0:T(1,128)S(1)}, u32[]{:S(2)}, u32[]{:S(2)}) collective-permute-start(f32[3,1,1,8,128]{4,2,3,1,0:T(1,128)S(1)} %pad_maximum_fusion.8), channel_id=1, source_target_pairs={{1,0},{2,1},{3,2},{4,3},{5,4},{6,5},{7,6},{9,8},{10,9},{11,10},{12... | collective-permute-start | bytes 36872 | tf_op jit(solution)/shard_map/ppermute | solution.py:17
  252.1 3.3 collective-permute-done.30
  262.9 2.4 collective-permute-start.32
  265.4 2.6 collective-permute-done.32
  268.0 3.7 %collective-permute-start.35 = (f32[3,1,4,8,128]{4,3,2,1,0:T(8,128)S(1)}, f32[3,1,4,8,128]{4,3,2,1,0:T(8,128)S(1)}, u32[]{:S(2)}, u32[]{:S(2)}) collective-permute-start(f32[3,1,4,8,128]{4,3,2,1,0:T(8,128)S(1)} %pad_maximum_fusion.2), channel_id=1, source_target_pairs={{1,0},{2,1},{3,2},{4,3},{5,4},{6,5},{7,6},{9,8},{10,9},{11,10},{12... | collective-permute-start | bytes 147464 | tf_op jit(solution)/shard_map/ppermute | solution.py:17
  273.9 4.7 %collective-permute-done.34 = f32[3,1,4,8,128]{4,3,2,1,0:T(8,128)S(1)} collective-permute-done((f32[3,1,4,8,128]{4,3,2,1,0:T(8,128)S(1)}, f32[3,1,4,8,128]{4,3,2,1,0:T(8,128)S(1)}, u32[]{:S(2)}, u32[]{:S(2)}) %collective-permute-start.34) | collective-permute-done | bytes 49184 | tf_op jit(solution)/shard_map/ppermute | solution.py:16
  280.1 3.8 %fusion.34 = f32[16,8,128]{2,1,0:T(8,128)S(1)} fusion(f32[16,4,8,128]{3,2,1,0:T(8,128)S(1)} %bitcast.470, f32[1,1,16,4,128,128]{5,4,3,2,1,0:T(8,128)} %param.38), kind=kOutput, calls=%fused_computation.54 | convolution fusion | flops 100663296 | bytes 4521984 | tf_op jit(solution)/shard_map/...bkrn,...bknm->...brm/dot_general | solution.py:63
  287.7 2.4 collective-permute-start.36
  290.1 2.6 collective-permute-done.36
  292.7 3.9 %collective-permute-start.39 = (f32[3,1,4,8,128]{4,3,2,1,0:T(8,128)S(1)}, f32[3,1,4,8,128]{4,3,2,1,0:T(8,128)S(1)}, u32[]{:S(2)}, u32[]{:S(2)}) collective-permute-start(f32[3,1,4,8,128]{4,3,2,1,0:T(8,128)S(1)} %pad_maximum_fusion.3), channel_id=1, source_target_pairs={{1,0},{2,1},{3,2},{4,3},{5,4},{6,5},{7,6},{9,8},{10,9},{11,10},{12... | collective-permute-start | bytes 147464 | tf_op jit(solution)/shard_map/ppermute | solution.py:17
  298.8 4.7 %collective-permute-done.38 = f32[3,1,4,8,128]{4,3,2,1,0:T(8,128)S(1)} collective-permute-done((f32[3,1,4,8,128]{4,3,2,1,0:T(8,128)S(1)}, f32[3,1,4,8,128]{4,3,2,1,0:T(8,128)S(1)}, u32[]{:S(2)}, u32[]{:S(2)}) %collective-permute-start.38) | collective-permute-done | bytes 49184 | tf_op jit(solution)/shard_map/ppermute | solution.py:16
  304.4 3.8 %fusion.37 = f32[16,8,128]{2,1,0:T(8,128)S(1)} fusion(f32[16,4,8,128]{3,2,1,0:T(8,128)S(1)} %bitcast.471, f32[1,1,16,4,128,128]{5,4,3,2,1,0:T(8,128)} %param.38), kind=kOutput, calls=%fused_computation.55 | convolution fusion | flops 100663296 | bytes 4521984 | tf_op jit(solution)/shard_map/...bkrn,...bknm->...brm/dot_general | solution.py:63
  312.6 2.4 collective-permute-start.40
  315.0 2.6 collective-permute-done.40
  319.6 3.9 %collective-permute-start.42 = (f32[3,1,4,8,128]{4,3,2,1,0:T(8,128)S(1)}, f32[3,1,4,8,128]{4,3,2,1,0:T(8,128)S(1)}, u32[]{:S(2)}, u32[]{:S(2)}) collective-permute-start(f32[3,1,4,8,128]{4,3,2,1,0:T(8,128)S(1)} %pad_maximum_fusion.4), channel_id=1, source_target_pairs={{0,1},{1,2},{2,3},{3,4},{4,5},{5,6},{6,7},{8,9},{9,10},{10,11},{11... | collective-permute-start | bytes 147464 | tf_op jit(solution)/shard_map/ppermute | solution.py:16
  323.5 2.9 collective-permute-done.42
  327.4 3.8 %fusion.40 = f32[16,8,128]{2,1,0:T(8,128)S(1)} fusion(f32[16,4,8,128]{3,2,1,0:T(8,128)S(1)} %bitcast.467, f32[1,1,16,4,128,128]{5,4,3,2,1,0:T(8,128)} %param.38), kind=kOutput, calls=%fused_computation.56 | convolution fusion | flops 100663296 | bytes 4521984 | tf_op jit(solution)/shard_map/...bkrn,...bknm->...brm/dot_general | solution.py:63
  (246 shorter events, 137.7 us)
Async XLA Ops:
  7.1 9.9 %collective-permute-start.1 = (f32[1,1,4,8,128]{4,3,2,1,0:T(8,128)S(1)}, f32[1,1,4,8,128]{4,3,2,1,0:T(8,128)S(1)}, u32[]{:S(2)}, u32[]{:S(2)}) collective-permute-start(f32[1,1,4,8,128]{4,3,2,1,0:T(8,128)S(1)} %bitcast_select_fusion.17), channel_id=1, source_target_pairs={{8,0},{16,8},{24,16},{9,1},{17,9},{25,17},{10,2},{18,10},{26,18},{... | collective-permute-start | bytes 49160 | tf_op jit(solution)/shard_map/ppermute | solution.py:17
  9.0 8.0 %collective-permute-start = (f32[1,1,4,8,128]{4,3,2,1,0:T(8,128)S(1)}, f32[1,1,4,8,128]{4,3,2,1,0:T(8,128)S(1)}, u32[]{:S(2)}, u32[]{:S(2)}) collective-permute-start(f32[1,1,4,8,128]{4,3,2,1,0:T(8,128)S(1)} %bitcast_select_fusion.17), channel_id=1, source_target_pairs={{0,8},{8,16},{16,24},{1,9},{9,17},{17,25},{2,10},{10,18},{18,26},{... | collective-permute-start | bytes 49160 | tf_op jit(solution)/shard_map/ppermute | solution.py:16
  17.0 10.2 %collective-permute-start.3 = (f32[3,1,4,8,128]{4,3,2,1,0:T(8,128)S(1)}, f32[3,1,4,8,128]{4,3,2,1,0:T(8,128)S(1)}, u32[]{:S(2)}, u32[]{:S(2)}) collective-permute-start(f32[3,1,4,8,128]{4,3,2,1,0:T(8,128)S(1)} %pad_maximum_fusion), channel_id=1, source_target_pairs={{1,0},{2,1},{3,2},{4,3},{5,4},{6,5},{7,6},{9,8},{10,9},{11,10},{12... | collective-permute-start | bytes 147464 | tf_op jit(solution)/shard_map/ppermute | solution.py:17
  20.3 6.9 %collective-permute-start.2 = (f32[3,1,4,8,128]{4,3,2,1,0:T(8,128)S(1)}, f32[3,1,4,8,128]{4,3,2,1,0:T(8,128)S(1)}, u32[]{:S(2)}, u32[]{:S(2)}) collective-permute-start(f32[3,1,4,8,128]{4,3,2,1,0:T(8,128)S(1)} %pad_maximum_fusion), channel_id=1, source_target_pairs={{0,1},{1,2},{2,3},{3,4},{4,5},{5,6},{6,7},{8,9},{9,10},{10,11},{11... | collective-permute-start | bytes 147464 | tf_op jit(solution)/shard_map/ppermute | solution.py:16
  33.6 6.9 %collective-permute-start.5 = (f32[1,1,4,8,128]{4,3,2,1,0:T(8,128)S(1)}, f32[1,1,4,8,128]{4,3,2,1,0:T(8,128)S(1)}, u32[]{:S(2)}, u32[]{:S(2)}) collective-permute-start(f32[1,1,4,8,128]{4,3,2,1,0:T(8,128)S(1)} %bitcast_select_fusion.16), channel_id=1, source_target_pairs={{8,0},{16,8},{24,16},{9,1},{17,9},{25,17},{10,2},{18,10},{26,18},{... | collective-permute-start | bytes 49160 | tf_op jit(solution)/shard_map/ppermute | solution.py:17
  36.0 5.1 %collective-permute-start.4 = (f32[1,1,4,8,128]{4,3,2,1,0:T(8,128)S(1)}, f32[1,1,4,8,128]{4,3,2,1,0:T(8,128)S(1)}, u32[]{:S(2)}, u32[]{:S(2)}) collective-permute-start(f32[1,1,4,8,128]{4,3,2,1,0:T(8,128)S(1)} %bitcast_select_fusion.16), channel_id=1, source_target_pairs={{0,8},{8,16},{16,24},{1,9},{9,17},{17,25},{2,10},{10,18},{18,26},{... | collective-permute-start | bytes 49160 | tf_op jit(solution)/shard_map/ppermute | solution.py:16
  41.1 8.8 %collective-permute-start.7 = (f32[3,1,4,8,128]{4,3,2,1,0:T(8,128)S(1)}, f32[3,1,4,8,128]{4,3,2,1,0:T(8,128)S(1)}, u32[]{:S(2)}, u32[]{:S(2)}) collective-permute-start(f32[3,1,4,8,128]{4,3,2,1,0:T(8,128)S(1)} %pad_maximum_fusion.1), channel_id=1, source_target_pairs={{1,0},{2,1},{3,2},{4,3},{5,4},{6,5},{7,6},{9,8},{10,9},{11,10},{12... | collective-permute-start | bytes 147464 | tf_op jit(solution)/shard_map/ppermute | solution.py:17
  43.0 6.9 %collective-permute-start.6 = (f32[3,1,4,8,128]{4,3,2,1,0:T(8,128)S(1)}, f32[3,1,4,8,128]{4,3,2,1,0:T(8,128)S(1)}, u32[]{:S(2)}, u32[]{:S(2)}) collective-permute-start(f32[3,1,4,8,128]{4,3,2,1,0:T(8,128)S(1)} %pad_maximum_fusion.1), channel_id=1, source_target_pairs={{0,1},{1,2},{2,3},{3,4},{4,5},{5,6},{6,7},{8,9},{9,10},{10,11},{11... | collective-permute-start | bytes 147464 | tf_op jit(solution)/shard_map/ppermute | solution.py:16
  55.7 99.5 %copy-start.4 = (f32[1,4,128,128]{3,2,1,0:T(8,128)S(1)}, f32[1,4,128,128]{3,2,1,0:T(8,128)}, u32[]{:S(2)}) copy-start(f32[1,4,128,128]{3,2,1,0:T(8,128)} %param.49) | copy-start | bytes 786436
  55.7 105.6 %copy-start.1 = (f32[1,4,4,128,128]{4,3,2,1,0:T(8,128)S(1)}, f32[1,4,4,128,128]{4,3,2,1,0:T(8,128)}, u32[]{:S(2)}) copy-start(f32[1,4,4,128,128]{4,3,2,1,0:T(8,128)} %param.50) | copy-start | bytes 3145732
  60.1 60.1 %copy-start.8 = (f32[4,8,128]{2,0,1:T(4,128)}, f32[4,8,128]{2,0,1:T(4,128)S(1)}, u32[]{:S(2)}) copy-start(f32[4,8,128]{2,0,1:T(4,128)S(1)} %get-tuple-element.45) | copy-start | bytes 49156
  60.8 7.7 %collective-permute-start.9 = (f32[1,1,1,8,128]{4,2,3,1,0:T(1,128)}, f32[1,1,1,8,128]{4,2,3,1,0:T(1,128)}, u32[]{:S(2)}, u32[]{:S(2)}) collective-permute-start(f32[1,1,1,8,128]{4,2,3,1,0:T(1,128)} %broadcast_select_fusion.3), channel_id=1, source_target_pairs={{8,0},{16,8},{24,16},{9,1},{17,9},{25,17},{10,2},{18,10},{26,18},{... | collective-permute-start | bytes 12296 | tf_op jit(solution)/shard_map/ppermute | solution.py:17
  63.0 5.4 %collective-permute-start.8 = (f32[1,1,1,8,128]{4,2,3,1,0:T(1,128)}, f32[1,1,1,8,128]{4,2,3,1,0:T(1,128)}, u32[]{:S(2)}, u32[]{:S(2)}) collective-permute-start(f32[1,1,1,8,128]{4,2,3,1,0:T(1,128)} %broadcast_select_fusion.3), channel_id=1, source_target_pairs={{0,8},{8,16},{16,24},{1,9},{9,17},{17,25},{2,10},{10,18},{18,26},{... | collective-permute-start | bytes 12296 | tf_op jit(solution)/shard_map/ppermute | solution.py:16
  69.1 7.7 %collective-permute-start.11 = (f32[3,1,1,8,128]{4,2,3,1,0:T(1,128)S(1)}, f32[3,1,1,8,128]{4,2,3,1,0:T(1,128)S(1)}, u32[]{:S(2)}, u32[]{:S(2)}) collective-permute-start(f32[3,1,1,8,128]{4,2,3,1,0:T(1,128)S(1)} %pad_maximum_fusion.5), channel_id=1, source_target_pairs={{1,0},{2,1},{3,2},{4,3},{5,4},{6,5},{7,6},{9,8},{10,9},{11,10},{12... | collective-permute-start | bytes 36872 | tf_op jit(solution)/shard_map/ppermute | solution.py:17
  72.1 6.5 %collective-permute-start.10 = (f32[3,1,1,8,128]{4,2,3,1,0:T(1,128)S(1)}, f32[3,1,1,8,128]{4,2,3,1,0:T(1,128)S(1)}, u32[]{:S(2)}, u32[]{:S(2)}) collective-permute-start(f32[3,1,1,8,128]{4,2,3,1,0:T(1,128)S(1)} %pad_maximum_fusion.5), channel_id=1, source_target_pairs={{0,1},{1,2},{2,3},{3,4},{4,5},{5,6},{6,7},{8,9},{9,10},{10,11},{11... | collective-permute-start | bytes 36872 | tf_op jit(solution)/shard_map/ppermute | solution.py:16
  87.5 12.2 %collective-permute-start.13 = (f32[1,1,1,8,128]{4,2,3,1,0:T(1,128)}, f32[1,1,1,8,128]{4,2,3,1,0:T(1,128)}, u32[]{:S(2)}, u32[]{:S(2)}) collective-permute-start(f32[1,1,1,8,128]{4,2,3,1,0:T(1,128)} %broadcast_select_fusion.2), channel_id=1, source_target_pairs={{8,0},{16,8},{24,16},{9,1},{17,9},{25,17},{10,2},{18,10},{26,18},{... | collective-permute-start | bytes 12296 | tf_op jit(solution)/shard_map/ppermute | solution.py:17
  89.4 10.3 %collective-permute-start.12 = (f32[1,1,1,8,128]{4,2,3,1,0:T(1,128)}, f32[1,1,1,8,128]{4,2,3,1,0:T(1,128)}, u32[]{:S(2)}, u32[]{:S(2)}) collective-permute-start(f32[1,1,1,8,128]{4,2,3,1,0:T(1,128)} %broadcast_select_fusion.2), channel_id=1, source_target_pairs={{0,8},{8,16},{16,24},{1,9},{9,17},{17,25},{2,10},{10,18},{18,26},{... | collective-permute-start | bytes 12296 | tf_op jit(solution)/shard_map/ppermute | solution.py:16
  100.4 7.8 %collective-permute-start.15 = (f32[3,1,1,8,128]{4,2,3,1,0:T(1,128)S(1)}, f32[3,1,1,8,128]{4,2,3,1,0:T(1,128)S(1)}, u32[]{:S(2)}, u32[]{:S(2)}) collective-permute-start(f32[3,1,1,8,128]{4,2,3,1,0:T(1,128)S(1)} %pad_maximum_fusion.6), channel_id=1, source_target_pairs={{1,0},{2,1},{3,2},{4,3},{5,4},{6,5},{7,6},{9,8},{10,9},{11,10},{12... | collective-permute-start | bytes 36872 | tf_op jit(solution)/shard_map/ppermute | solution.py:17
  103.1 6.5 %collective-permute-start.14 = (f32[3,1,1,8,128]{4,2,3,1,0:T(1,128)S(1)}, f32[3,1,1,8,128]{4,2,3,1,0:T(1,128)S(1)}, u32[]{:S(2)}, u32[]{:S(2)}) collective-permute-start(f32[3,1,1,8,128]{4,2,3,1,0:T(1,128)S(1)} %pad_maximum_fusion.6), channel_id=1, source_target_pairs={{0,1},{1,2},{2,3},{3,4},{4,5},{5,6},{6,7},{8,9},{9,10},{10,11},{11... | collective-permute-start | bytes 36872 | tf_op jit(solution)/shard_map/ppermute | solution.py:16
  150.8 5.3 %collective-permute-start.17 = (f32[1,1,8,128]{3,2,1,0:T(8,128)S(1)}, f32[1,1,8,128]{3,2,1,0:T(8,128)S(1)}, u32[]{:S(2)}, u32[]{:S(2)}) collective-permute-start(f32[1,1,8,128]{3,2,1,0:T(8,128)S(1)} %dynamic-slice_select_fusion.3), channel_id=1, source_target_pairs={{8,0},{16,8},{24,16},{9,1},{17,9},{25,17},{10,2},{18,10},{26,18},{... | collective-permute-start | bytes 12296 | tf_op jit(solution)/shard_map/ppermute | solution.py:17
  152.8 4.9 %collective-permute-start.16 = (f32[1,1,8,128]{3,2,1,0:T(8,128)S(1)}, f32[1,1,8,128]{3,2,1,0:T(8,128)S(1)}, u32[]{:S(2)}, u32[]{:S(2)}) collective-permute-start(f32[1,1,8,128]{3,2,1,0:T(8,128)S(1)} %dynamic-slice_select_fusion.3), channel_id=1, source_target_pairs={{0,8},{8,16},{16,24},{1,9},{9,17},{17,25},{2,10},{10,18},{18,26},{... | collective-permute-start | bytes 12296 | tf_op jit(solution)/shard_map/ppermute | solution.py:16
  163.2 5.4 %collective-permute-start.19 = (f32[1,1,8,128]{3,2,1,0:T(8,128)S(1)}, f32[1,1,8,128]{3,2,1,0:T(8,128)S(1)}, u32[]{:S(2)}, u32[]{:S(2)}) collective-permute-start(f32[1,1,8,128]{3,2,1,0:T(8,128)S(1)} %dynamic-slice_select_fusion.2), channel_id=1, source_target_pairs={{8,0},{16,8},{24,16},{9,1},{17,9},{25,17},{10,2},{18,10},{26,18},{... | collective-permute-start | bytes 12296 | tf_op jit(solution)/shard_map/ppermute | solution.py:17
  165.2 4.9 %collective-permute-start.18 = (f32[1,1,8,128]{3,2,1,0:T(8,128)S(1)}, f32[1,1,8,128]{3,2,1,0:T(8,128)S(1)}, u32[]{:S(2)}, u32[]{:S(2)}) collective-permute-start(f32[1,1,8,128]{3,2,1,0:T(8,128)S(1)} %dynamic-slice_select_fusion.2), channel_id=1, source_target_pairs={{0,8},{8,16},{16,24},{1,9},{9,17},{17,25},{2,10},{10,18},{18,26},{... | collective-permute-start | bytes 12296 | tf_op jit(solution)/shard_map/ppermute | solution.py:16
  193.7 5.3 %collective-permute-start.21 = (f32[1,1,8,128]{3,2,1,0:T(8,128)S(1)}, f32[1,1,8,128]{3,2,1,0:T(8,128)S(1)}, u32[]{:S(2)}, u32[]{:S(2)}) collective-permute-start(f32[1,1,8,128]{3,2,1,0:T(8,128)S(1)} %dynamic-slice_select_fusion.1), channel_id=1, source_target_pairs={{8,0},{16,8},{24,16},{9,1},{17,9},{25,17},{10,2},{18,10},{26,18},{... | collective-permute-start | bytes 12296 | tf_op jit(solution)/shard_map/ppermute | solution.py:17
  195.6 4.9 %collective-permute-start.20 = (f32[1,1,8,128]{3,2,1,0:T(8,128)S(1)}, f32[1,1,8,128]{3,2,1,0:T(8,128)S(1)}, u32[]{:S(2)}, u32[]{:S(2)}) collective-permute-start(f32[1,1,8,128]{3,2,1,0:T(8,128)S(1)} %dynamic-slice_select_fusion.1), channel_id=1, source_target_pairs={{0,8},{8,16},{16,24},{1,9},{9,17},{17,25},{2,10},{10,18},{18,26},{... | collective-permute-start | bytes 12296 | tf_op jit(solution)/shard_map/ppermute | solution.py:16
  205.5 52.0 %copy-start.10 = (f32[4,8,128]{2,0,1:T(4,128)S(1)}, f32[4,8,128]{2,0,1:T(4,128)}, u32[]{:S(2)}) copy-start(f32[4,8,128]{2,0,1:T(4,128)} %get-tuple-element.46) | copy-start | bytes 49156
  205.5 5.3 %collective-permute-start.23 = (f32[1,1,8,128]{3,2,1,0:T(8,128)S(1)}, f32[1,1,8,128]{3,2,1,0:T(8,128)S(1)}, u32[]{:S(2)}, u32[]{:S(2)}) collective-permute-start(f32[1,1,8,128]{3,2,1,0:T(8,128)S(1)} %dynamic-slice_select_fusion), channel_id=1, source_target_pairs={{8,0},{16,8},{24,16},{9,1},{17,9},{25,17},{10,2},{18,10},{26,18},{... | collective-permute-start | bytes 12296 | tf_op jit(solution)/shard_map/ppermute | solution.py:17
  207.5 4.9 %collective-permute-start.22 = (f32[1,1,8,128]{3,2,1,0:T(8,128)S(1)}, f32[1,1,8,128]{3,2,1,0:T(8,128)S(1)}, u32[]{:S(2)}, u32[]{:S(2)}) collective-permute-start(f32[1,1,8,128]{3,2,1,0:T(8,128)S(1)} %dynamic-slice_select_fusion), channel_id=1, source_target_pairs={{0,8},{8,16},{16,24},{1,9},{9,17},{17,25},{2,10},{10,18},{18,26},{... | collective-permute-start | bytes 12296 | tf_op jit(solution)/shard_map/ppermute | solution.py:16
  218.2 4.3 %collective-permute-start.25 = (f32[1,1,1,8,128]{4,2,3,1,0:T(1,128)S(1)}, f32[1,1,1,8,128]{4,2,3,1,0:T(1,128)S(1)}, u32[]{:S(2)}, u32[]{:S(2)}) collective-permute-start(f32[1,1,1,8,128]{4,2,3,1,0:T(1,128)S(1)} %broadcast_select_fusion.1), channel_id=1, source_target_pairs={{8,0},{16,8},{24,16},{9,1},{17,9},{25,17},{10,2},{18,10},{26,18},{... | collective-permute-start | bytes 12296 | tf_op jit(solution)/shard_map/ppermute | solution.py:17
  220.1 4.9 %collective-permute-start.24 = (f32[1,1,1,8,128]{4,2,3,1,0:T(1,128)S(1)}, f32[1,1,1,8,128]{4,2,3,1,0:T(1,128)S(1)}, u32[]{:S(2)}, u32[]{:S(2)}) collective-permute-start(f32[1,1,1,8,128]{4,2,3,1,0:T(1,128)S(1)} %broadcast_select_fusion.1), channel_id=1, source_target_pairs={{0,8},{8,16},{16,24},{1,9},{9,17},{17,25},{2,10},{10,18},{18,26},{... | collective-permute-start | bytes 12296 | tf_op jit(solution)/shard_map/ppermute | solution.py:16
  225.0 7.1 %collective-permute-start.27 = (f32[3,1,1,8,128]{4,2,3,1,0:T(1,128)S(1)}, f32[3,1,1,8,128]{4,2,3,1,0:T(1,128)S(1)}, u32[]{:S(2)}, u32[]{:S(2)}) collective-permute-start(f32[3,1,1,8,128]{4,2,3,1,0:T(1,128)S(1)} %pad_maximum_fusion.7), channel_id=1, source_target_pairs={{1,0},{2,1},{3,2},{4,3},{5,4},{6,5},{7,6},{9,8},{10,9},{11,10},{12... | collective-permute-start | bytes 36872 | tf_op jit(solution)/shard_map/ppermute | solution.py:17
  227.6 7.7 %collective-permute-start.26 = (f32[3,1,1,8,128]{4,2,3,1,0:T(1,128)S(1)}, f32[3,1,1,8,128]{4,2,3,1,0:T(1,128)S(1)}, u32[]{:S(2)}, u32[]{:S(2)}) collective-permute-start(f32[3,1,1,8,128]{4,2,3,1,0:T(1,128)S(1)} %pad_maximum_fusion.7), channel_id=1, source_target_pairs={{0,1},{1,2},{2,3},{3,4},{4,5},{5,6},{6,7},{8,9},{9,10},{10,11},{11... | collective-permute-start | bytes 36872 | tf_op jit(solution)/shard_map/ppermute | solution.py:16
  238.1 4.3 %collective-permute-start.29 = (f32[1,1,1,8,128]{4,2,3,1,0:T(1,128)S(1)}, f32[1,1,1,8,128]{4,2,3,1,0:T(1,128)S(1)}, u32[]{:S(2)}, u32[]{:S(2)}) collective-permute-start(f32[1,1,1,8,128]{4,2,3,1,0:T(1,128)S(1)} %broadcast_select_fusion), channel_id=1, source_target_pairs={{8,0},{16,8},{24,16},{9,1},{17,9},{25,17},{10,2},{18,10},{26,18},{... | collective-permute-start | bytes 12296 | tf_op jit(solution)/shard_map/ppermute | solution.py:17
  240.1 4.9 %collective-permute-start.28 = (f32[1,1,1,8,128]{4,2,3,1,0:T(1,128)S(1)}, f32[1,1,1,8,128]{4,2,3,1,0:T(1,128)S(1)}, u32[]{:S(2)}, u32[]{:S(2)}) collective-permute-start(f32[1,1,1,8,128]{4,2,3,1,0:T(1,128)S(1)} %broadcast_select_fusion), channel_id=1, source_target_pairs={{0,8},{8,16},{16,24},{1,9},{9,17},{17,25},{2,10},{10,18},{18,26},{... | collective-permute-start | bytes 12296 | tf_op jit(solution)/shard_map/ppermute | solution.py:16
  245.0 7.1 %collective-permute-start.31 = (f32[3,1,1,8,128]{4,2,3,1,0:T(1,128)S(1)}, f32[3,1,1,8,128]{4,2,3,1,0:T(1,128)S(1)}, u32[]{:S(2)}, u32[]{:S(2)}) collective-permute-start(f32[3,1,1,8,128]{4,2,3,1,0:T(1,128)S(1)} %pad_maximum_fusion.8), channel_id=1, source_target_pairs={{1,0},{2,1},{3,2},{4,3},{5,4},{6,5},{7,6},{9,8},{10,9},{11,10},{12... | collective-permute-start | bytes 36872 | tf_op jit(solution)/shard_map/ppermute | solution.py:17
  248.9 6.5 %collective-permute-start.30 = (f32[3,1,1,8,128]{4,2,3,1,0:T(1,128)S(1)}, f32[3,1,1,8,128]{4,2,3,1,0:T(1,128)S(1)}, u32[]{:S(2)}, u32[]{:S(2)}) collective-permute-start(f32[3,1,1,8,128]{4,2,3,1,0:T(1,128)S(1)} %pad_maximum_fusion.8), channel_id=1, source_target_pairs={{0,1},{1,2},{2,3},{3,4},{4,5},{5,6},{6,7},{8,9},{9,10},{10,11},{11... | collective-permute-start | bytes 36872 | tf_op jit(solution)/shard_map/ppermute | solution.py:16
  261.0 4.3 %collective-permute-start.33 = (f32[1,1,4,8,128]{4,3,2,1,0:T(8,128)S(1)}, f32[1,1,4,8,128]{4,3,2,1,0:T(8,128)S(1)}, u32[]{:S(2)}, u32[]{:S(2)}) collective-permute-start(f32[1,1,4,8,128]{4,3,2,1,0:T(8,128)S(1)} %bitcast_select_fusion.15), channel_id=1, source_target_pairs={{8,0},{16,8},{24,16},{9,1},{17,9},{25,17},{10,2},{18,10},{26,18},{... | collective-permute-start | bytes 49160 | tf_op jit(solution)/shard_map/ppermute | solution.py:17
  262.9 5.1 %collective-permute-start.32 = (f32[1,1,4,8,128]{4,3,2,1,0:T(8,128)S(1)}, f32[1,1,4,8,128]{4,3,2,1,0:T(8,128)S(1)}, u32[]{:S(2)}, u32[]{:S(2)}) collective-permute-start(f32[1,1,4,8,128]{4,3,2,1,0:T(8,128)S(1)} %bitcast_select_fusion.15), channel_id=1, source_target_pairs={{0,8},{8,16},{16,24},{1,9},{9,17},{17,25},{2,10},{10,18},{18,26},{... | collective-permute-start | bytes 49160 | tf_op jit(solution)/shard_map/ppermute | solution.py:16
  268.0 10.6 %collective-permute-start.35 = (f32[3,1,4,8,128]{4,3,2,1,0:T(8,128)S(1)}, f32[3,1,4,8,128]{4,3,2,1,0:T(8,128)S(1)}, u32[]{:S(2)}, u32[]{:S(2)}) collective-permute-start(f32[3,1,4,8,128]{4,3,2,1,0:T(8,128)S(1)} %pad_maximum_fusion.2), channel_id=1, source_target_pairs={{1,0},{2,1},{3,2},{4,3},{5,4},{6,5},{7,6},{9,8},{10,9},{11,10},{12... | collective-permute-start | bytes 147464 | tf_op jit(solution)/shard_map/ppermute | solution.py:17
  271.7 6.9 %collective-permute-start.34 = (f32[3,1,4,8,128]{4,3,2,1,0:T(8,128)S(1)}, f32[3,1,4,8,128]{4,3,2,1,0:T(8,128)S(1)}, u32[]{:S(2)}, u32[]{:S(2)}) collective-permute-start(f32[3,1,4,8,128]{4,3,2,1,0:T(8,128)S(1)} %pad_maximum_fusion.2), channel_id=1, source_target_pairs={{0,1},{1,2},{2,3},{3,4},{4,5},{5,6},{6,7},{8,9},{9,10},{10,11},{11... | collective-permute-start | bytes 147464 | tf_op jit(solution)/shard_map/ppermute | solution.py:16
  285.7 4.3 %collective-permute-start.37 = (f32[1,1,4,8,128]{4,3,2,1,0:T(8,128)S(1)}, f32[1,1,4,8,128]{4,3,2,1,0:T(8,128)S(1)}, u32[]{:S(2)}, u32[]{:S(2)}) collective-permute-start(f32[1,1,4,8,128]{4,3,2,1,0:T(8,128)S(1)} %bitcast_select_fusion.14), channel_id=1, source_target_pairs={{8,0},{16,8},{24,16},{9,1},{17,9},{25,17},{10,2},{18,10},{26,18},{... | collective-permute-start | bytes 49160 | tf_op jit(solution)/shard_map/ppermute | solution.py:17
  287.7 5.1 %collective-permute-start.36 = (f32[1,1,4,8,128]{4,3,2,1,0:T(8,128)S(1)}, f32[1,1,4,8,128]{4,3,2,1,0:T(8,128)S(1)}, u32[]{:S(2)}, u32[]{:S(2)}) collective-permute-start(f32[1,1,4,8,128]{4,3,2,1,0:T(8,128)S(1)} %bitcast_select_fusion.14), channel_id=1, source_target_pairs={{0,8},{8,16},{16,24},{1,9},{9,17},{17,25},{2,10},{10,18},{18,26},{... | collective-permute-start | bytes 49160 | tf_op jit(solution)/shard_map/ppermute | solution.py:16
  292.7 10.8 %collective-permute-start.39 = (f32[3,1,4,8,128]{4,3,2,1,0:T(8,128)S(1)}, f32[3,1,4,8,128]{4,3,2,1,0:T(8,128)S(1)}, u32[]{:S(2)}, u32[]{:S(2)}) collective-permute-start(f32[3,1,4,8,128]{4,3,2,1,0:T(8,128)S(1)} %pad_maximum_fusion.3), channel_id=1, source_target_pairs={{1,0},{2,1},{3,2},{4,3},{5,4},{6,5},{7,6},{9,8},{10,9},{11,10},{12... | collective-permute-start | bytes 147464 | tf_op jit(solution)/shard_map/ppermute | solution.py:17
  296.6 6.9 %collective-permute-start.38 = (f32[3,1,4,8,128]{4,3,2,1,0:T(8,128)S(1)}, f32[3,1,4,8,128]{4,3,2,1,0:T(8,128)S(1)}, u32[]{:S(2)}, u32[]{:S(2)}) collective-permute-start(f32[3,1,4,8,128]{4,3,2,1,0:T(8,128)S(1)} %pad_maximum_fusion.3), channel_id=1, source_target_pairs={{0,1},{1,2},{2,3},{3,4},{4,5},{5,6},{6,7},{8,9},{9,10},{10,11},{11... | collective-permute-start | bytes 147464 | tf_op jit(solution)/shard_map/ppermute | solution.py:16
  310.7 4.3 %collective-permute-start.41 = (f32[1,1,4,8,128]{4,3,2,1,0:T(8,128)S(1)}, f32[1,1,4,8,128]{4,3,2,1,0:T(8,128)S(1)}, u32[]{:S(2)}, u32[]{:S(2)}) collective-permute-start(f32[1,1,4,8,128]{4,3,2,1,0:T(8,128)S(1)} %bitcast_select_fusion.13), channel_id=1, source_target_pairs={{8,0},{16,8},{24,16},{9,1},{17,9},{25,17},{10,2},{18,10},{26,18},{... | collective-permute-start | bytes 49160 | tf_op jit(solution)/shard_map/ppermute | solution.py:17
  312.6 5.1 %collective-permute-start.40 = (f32[1,1,4,8,128]{4,3,2,1,0:T(8,128)S(1)}, f32[1,1,4,8,128]{4,3,2,1,0:T(8,128)S(1)}, u32[]{:S(2)}, u32[]{:S(2)}) collective-permute-start(f32[1,1,4,8,128]{4,3,2,1,0:T(8,128)S(1)} %bitcast_select_fusion.13), channel_id=1, source_target_pairs={{0,8},{8,16},{16,24},{1,9},{9,17},{17,25},{2,10},{10,18},{18,26},{... | collective-permute-start | bytes 49160 | tf_op jit(solution)/shard_map/ppermute | solution.py:16
  317.7 8.8 %collective-permute-start.43 = (f32[3,1,4,8,128]{4,3,2,1,0:T(8,128)S(1)}, f32[3,1,4,8,128]{4,3,2,1,0:T(8,128)S(1)}, u32[]{:S(2)}, u32[]{:S(2)}) collective-permute-start(f32[3,1,4,8,128]{4,3,2,1,0:T(8,128)S(1)} %pad_maximum_fusion.4), channel_id=1, source_target_pairs={{1,0},{2,1},{3,2},{4,3},{5,4},{6,5},{7,6},{9,8},{10,9},{11,10},{12... | collective-permute-start | bytes 147464 | tf_op jit(solution)/shard_map/ppermute | solution.py:17
  319.6 6.9 %collective-permute-start.42 = (f32[3,1,4,8,128]{4,3,2,1,0:T(8,128)S(1)}, f32[3,1,4,8,128]{4,3,2,1,0:T(8,128)S(1)}, u32[]{:S(2)}, u32[]{:S(2)}) collective-permute-start(f32[3,1,4,8,128]{4,3,2,1,0:T(8,128)S(1)} %pad_maximum_fusion.4), channel_id=1, source_target_pairs={{0,1},{1,2},{2,3},{3,4},{4,5},{5,6},{6,7},{8,9},{9,10},{10,11},{11... | collective-permute-start | bytes 147464 | tf_op jit(solution)/shard_map/ppermute | solution.py:16
  (17 other events, 503.5 us)
where the time goes:
time: 336 us; the launch traced here: 333 us
  starting transfers between devices  110 us (33%)
  matrix products  60.8 us (18%)
  waiting for transfers between devices  47.7 us (14%)
  blocking collectives  41.9 us (12%)
  local copies, waits for them, and re-layouts  35.4 us (11%)
  other arithmetic  24.7 us (7%)
  between operations  12.2 us (4%)
    ppermute x22, starting transfers between devices, padded_2(): before = lax.ppermute(last, axis, up)  57.6 us
    ppermute x22, starting transfers between devices, padded_2(): after = lax.ppermute(initial, axis, down)  52.6 us
    ppermute x22, waiting for transfers between devices, padded_2(): before = lax.ppermute(last, axis, up)  47.6 us
    psum x1, blocking collectives, body(): row_target = lax.psum(row_share[:, 0], 'py')  30.6 us
    dot_general x13, matrix products, block_apply(): jnp.einsum('...bkrn,...bknm->...brm', picked, coupling, precision=HIGHEST)  27.7 us
    gather x13, local copies, waits for them, and re-layouts, block_apply(): jnp.take_along_axis(extended, flat_links[..., None, None], axis=lead_dims)  15.8 us
    dot_general x13, matrix products, block_apply(): jnp.einsum('...brn,...bnm->...brm', vector, diagonal, precision=HIGHEST)  15.6 us
    psum x1, blocking collectives, body(): top_target = lax.psum(top_part, 'px')  11.3 us
  transfers between devices with their start and end apart: 44, of which 19 were waited for; matrix products, arithmetic and copies ran while one was open for 6% of the time, Pallas kernels for 0%

commit v1 on v0

v1 whole, which is shorter than its diff:
```python
import functools

import jax
import jax.numpy as jnp
from jax import lax
from jax.experimental import pallas as pl
from jax.experimental.pallas import tpu as pltpu
from jax.sharding import PartitionSpec as P

MESH = pl.DeviceIdType.MESH
F32 = jnp.float32
BF16 = jnp.bfloat16


def halves(x):
    high = x.astype(BF16).astype(F32)
    return high, x - high


def rows_split(x):
    high, low = halves(x)
    return jnp.concatenate([high, low], axis=-2).astype(BF16)


def quarters(z):
    rows, cols = z.shape[0] // 2, z.shape[1] // 2
    folded = z[:, :cols] + z[:, cols:]
    return folded[:rows] + folded[rows:]


def kernel(
    npx,
    npy,
    live,
    links_fine,
    send_fine,
    owner_fine,
    links_mid,
    send_mid,
    owner_mid,
    links_row,
    send_row,
    owner_row,
    cheb_low,
    cheb_high,
    right_side,
    diag_fine,
    couple_fine,
    prolong_fine,
    diag_mid,
    couple_mid,
    prolong_mid,
    diag_row,
    couple_row,
    prolong_row,
    inverse,
    out_x,
    out_r,
    stage_df,
    stage_cf,
    stage_pf,
    stage_dm,
    stage_cm,
    stage_pm,
    stage_dr,
    stage_cr,
    stage_pr,
    stage_inv,
    w_df,
    w_cf,
    w_pf,
    w_dm,
    w_cm,
    w_pm,
    w_dr,
    w_cr,
    w_pr,
    w_inv,
    vec_f,
    ext_f,
    acc_f,
    vec_c,
    ext_c,
    acc_c,
    split_f,
    split_c,
    b_f,
    x_f,
    b_m,
    x_m,
    b_r,
    x_r,
    sbuf_f,
    rbuf_f,
    sbuf_m,
    rbuf_m,
    sbuf_r,
    rbuf_r,
    sum_y_src,
    sum_y,
    sum_x_src,
    sum_x,
    load_cf,
    load,
    ss_f,
    rs_f,
    ss_m,
    rs_m,
    ss_r,
    rs_r,
    ss_y,
    rs_y,
    ss_x,
    rs_x,
):
    px = lax.axis_index("px")
    py = lax.axis_index("py")
    fine = diag_fine.shape[0]
    mid = diag_mid.shape[0]
    row = diag_row.shape[0]
    node = diag_fine.shape[-1]
    top = inverse.shape[0] // node
    width_k = links_fine.shape[1]

    def couple_copy(b):
        return pltpu.make_async_copy(couple_fine.at[b], stage_cf.at[b], load_cf.at[b])

    def whole_copy(i):
        src, dst = (
            (diag_fine, stage_df),
            (prolong_fine, stage_pf),
            (diag_mid, stage_dm),
            (couple_mid, stage_cm),
            (prolong_mid, stage_pm),
            (diag_row, stage_dr),
            (couple_row, stage_cr),
            (prolong_row, stage_pr),
            (inverse, stage_inv),
        )[i]
        return pltpu.make_async_copy(src, dst, load.at[i])

    whole_copy(0).start()

    @pl.loop(0, fine)
    def _(b):
        couple_copy(b).start()

    for i in range(1, 9):
        whole_copy(i).start()

    barrier = pltpu.get_barrier_semaphore()
    for j in range(1, npx):
        pl.semaphore_signal(
            barrier, inc=1, device_id={"px": lax.rem(px + j, npx)}, device_id_type=MESH
        )
    for j in range(1, npy):
        pl.semaphore_signal(
            barrier, inc=1, device_id={"py": lax.rem(py + j, npy)}, device_id_type=MESH
        )

    has = (px > 0, px < npx - 1, py > 0, py < npy - 1)
    for d in range(4):

        @pl.when(jnp.logical_not(has[d]))
        def _(d=d):
            rbuf_f[:, d] = jnp.zeros(rbuf_f.shape[:1] + rbuf_f.shape[2:], F32)
            rbuf_m[:, d] = jnp.zeros(rbuf_m.shape[:1] + rbuf_m.shape[2:], F32)
            if d < 2:
                rbuf_r[:, d] = jnp.zeros(rbuf_r.shape[:1] + rbuf_r.shape[2:], F32)

    place = ({"px": px - 1}, {"px": px + 1}, {"py": py - 1}, {"py": py + 1})

    def halo_copy(bufs, e, d, target):
        src, dst, ss, rs = bufs
        return pltpu.make_async_remote_copy(
            src_ref=src.at[e],
            dst_ref=dst.at[e, d],
            send_sem=ss.at[e, d],
            recv_sem=rs.at[e, d],
            device_id=place[target],
            device_id_type=MESH,
        )

    def halo_start(bufs, e, dirs):
        for d in range(dirs):

            @pl.when(has[d ^ 1])
            def _(d=d):
                halo_copy(bufs, e, d, d ^ 1).start()

    def halo_recv(bufs, e, dirs):
        for d in range(dirs):

            @pl.when(has[d])
            def _(d=d):
                halo_copy(bufs, e, d, d).wait_recv()

    def halo_sent(bufs, count, dirs):
        for e in range(count):
            for d in range(dirs):

                @pl.when(has[d ^ 1])
                def _(d=d, e=e):
                    halo_copy(bufs, e, d, d ^ 1).wait_send()

    def sum_copy(axis, j):
        me, n, src, dst, ss, rs = (
            (px, npx, sum_x_src, sum_x, ss_x, rs_x)
            if axis == "px"
            else (py, npy, sum_y_src, sum_y, ss_y, rs_y)
        )
        return pltpu.make_async_remote_copy(
            src_ref=src,
            dst_ref=dst.at[j - 1],
            send_sem=ss.at[j - 1],
            recv_sem=rs.at[j - 1],
            device_id={axis: lax.rem(me + j, n)},
            device_id_type=MESH,
        )

    def all_sum(axis, n, src, dst, value):
        src[...] = value
        for j in range(1, n):
            sum_copy(axis, j).start()
        for j in range(1, n):
            sum_copy(axis, j).wait_recv()
        total = value
        for j in range(1, n):
            total = total + dst[j - 1]
        return total

    def split_cols(stage, w, b):
        high, low = halves(stage[b])
        w[b, :, :node] = high.astype(BF16)
        w[b, :, node:] = low.astype(BF16)

    def split_rows(stage, w, b):
        high, low = halves(stage[b])
        w[b, :node, :] = high.astype(BF16)
        w[b, node:, :] = low.astype(BF16)

    def split_all(i, stage, w, how):
        whole_copy(i).wait()

        @pl.loop(0, stage.shape[0])
        def _(b):
            how(stage, w, b)

    def split_couple_fine():
        @pl.loop(0, fine)
        def _(b):
            couple_copy(b).wait()
            split_cols(stage_cf, w_cf, b)

    def split_inverse():
        whole_copy(8).wait()
        size = inverse.shape[0]

        @pl.loop(0, size // node)
        def _(b):
            rows = pl.ds(pl.multiple_of(b * node, node), node)
            high, low = halves(stage_inv[rows, :])
            w_inv[rows, :size] = high.astype(BF16)
            w_inv[rows, size:] = low.astype(BF16)

    def apply(v, e, level, before_diag=None, before_couple=None):
        count, vec, ext, acc, bufs, dirs, links, send, w_d, w_c = level
        shared = send.shape[1]
        vec[:count] = v
        for h in range(shared):
            bufs[0][e, h] = vec[send[0, h]]
        halo_start(bufs, e, dirs)
        ext[:count] = rows_split(v)
        if before_diag is not None:
            before_diag()

        def own(b, carry):
            acc[b] = quarters(jnp.dot(ext[b], w_d[b], preferred_element_type=F32))
            return carry

        lax.fori_loop(0, count, own, 0, unroll=True)
        if before_couple is not None:
            before_couple()
        halo_recv(bufs, e, dirs)
        for d in range(dirs):
            ext[count + d * shared : count + (d + 1) * shared] = rows_split(bufs[1][e, d])

        def far(b, carry):
            picked = jnp.concatenate([ext[links[b, k]] for k in range(width_k)], axis=1)
            acc[b] += quarters(jnp.dot(picked, w_c[b], preferred_element_type=F32))
            return carry

        lax.fori_loop(0, count, far, 0, unroll=True)
        return acc[:count]

    def restrict(r, w_p, owner, count, groups, split):
        split[:count] = rows_split(r)
        totals = [jnp.zeros(r.shape[1:], F32) for _ in range(groups)]
        for b in range(count):
            piece = quarters(
                lax.dot_general(
                    split[b], w_p[b], (((1,), (1,)), ((), ())), preferred_element_type=F32
                )
            )
            for c in range(groups):
                totals[c] = totals[c] + piece * jnp.where(owner[0, b] == c, 1.0, 0.0)
        return jnp.stack(totals)

    def prolong(u, w_p, owner, count, split):
        split[: u.shape[0]] = rows_split(u)
        out = []
        for b in range(count):
            part = split[owner[0, b]]
            z = jnp.dot(
                jnp.concatenate([part, part], axis=1), w_p[b], preferred_element_type=F32
            )
            out.append(z[: z.shape[0] // 2] + z[z.shape[0] // 2 :])
        return jnp.stack(out)

    def terms(level):
        shape = right_side.shape[1:]
        low = jnp.full(shape, cheb_low[level], F32)
        high = jnp.full(shape, cheb_high[level], F32)
        center = 0.5 * (high + low)
        half_width = 0.5 * (high - low)
        ratio = center / half_width
        first = 1.0 / ratio
        second = 1.0 / (2.0 * ratio - first)
        return (1.0 / center)[None], (second * first)[None], (2.0 * second / half_width)[None]

    bufs_f = (sbuf_f, rbuf_f, ss_f, rs_f)
    bufs_m = (sbuf_m, rbuf_m, ss_m, rs_m)
    bufs_r = (sbuf_r, rbuf_r, ss_r, rs_r)
    level_f = (fine, vec_f, ext_f, acc_f, bufs_f, 4, links_fine, send_fine, w_df, w_cf)
    level_m = (mid, vec_c, ext_c, acc_c, bufs_m, 4, links_mid, send_mid, w_dm, w_cm)
    level_r = (row, vec_c, ext_c, acc_c, bufs_r, 2, links_row, send_row, w_dr, w_cr)

    mask = jnp.where(
        lax.broadcasted_iota(jnp.int32, right_side.shape, 0) < live[0, 0], 1.0, 0.0
    ).astype(F32)

    inv_c, carry_c, gain_c = terms(0)
    target = right_side[...] * mask
    b_f[...] = target
    d = target * inv_c
    pl.semaphore_wait(barrier, npx + npy - 2)
    ad = apply(
        d,
        0,
        level_f,
        before_diag=lambda: split_all(0, stage_df, w_df, split_cols),
        before_couple=split_couple_fine,
    )
    r = target - ad * mask
    d2 = carry_c * d + gain_c * r
    x_f[...] = d + d2

    def more():
        split_all(1, stage_pf, w_pf, split_rows)
        split_all(2, stage_dm, w_dm, split_cols)
        split_all(3, stage_cm, w_cm, split_cols)

    r = r - apply(d2, 1, level_f, before_couple=more) * mask

    inv_c, carry_c, gain_c = terms(1)
    target = restrict(r, w_pf, owner_fine, fine, mid, split_f)
    b_m[...] = target
    d = target * inv_c
    r = target - apply(
        d, 0, level_m, before_couple=lambda: split_all(4, stage_pm, w_pm, split_rows)
    )
    d2 = carry_c * d + gain_c * r
    x_m[...] = d + d2

    def row_split():
        split_all(5, stage_dr, w_dr, split_cols)
        split_all(6, stage_cr, w_cr, split_cols)
        split_all(7, stage_pr, w_pr, split_rows)

    r = r - apply(d2, 1, level_m, before_couple=row_split)

    inv_c, carry_c, gain_c = terms(2)
    share = restrict(r, w_pm, owner_mid, mid, row, split_c)
    target = all_sum("py", npy, sum_y_src, sum_y, share)
    b_r[...] = target
    d = target * inv_c
    r = target - apply(d, 0, level_r, before_couple=split_inverse)
    d2 = carry_c * d + gain_c * r
    x_r[...] = d + d2
    r = r - apply(d2, 1, level_r)

    part = restrict(r, w_pr, owner_row, row, top, split_c)
    top_target = all_sum("px", npx, sum_x_src, sum_x, part)
    flat = jnp.concatenate([rows_split(top_target[c]) for c in range(top)], axis=1)
    solved = quarters(jnp.dot(flat, w_inv[...], preferred_element_type=F32))
    top_sol = jnp.stack([solved[:, c * node : (c + 1) * node] for c in range(top)])

    x = x_r[...] + prolong(top_sol, w_pr, owner_row, row, split_c)
    x_r[...] = x
    r = b_r[...] - apply(x, 2, level_r)
    d = r * inv_c
    x_r[...] += d
    r = r - apply(d, 3, level_r)
    x = x_r[...] + carry_c * d + gain_c * r

    inv_c, carry_c, gain_c = terms(1)
    x = x_m[...] + prolong(x, w_pm, owner_mid, mid, split_c)
    x_m[...] = x
    r = b_m[...] - apply(x, 2, level_m)
    d = r * inv_c
    x_m[...] += d
    r = r - apply(d, 3, level_m)
    x = x_m[...] + carry_c * d + gain_c * r

    inv_c, carry_c, gain_c = terms(0)
    x = x_f[...] + prolong(x, w_pf, owner_fine, fine, split_c) * mask
    x_f[...] = x
    r = b_f[...] - apply(x, 2, level_f) * mask
    d = r * inv_c
    x_f[...] += d
    r = r - apply(d, 3, level_f) * mask
    d2 = carry_c * d + gain_c * r
    out_x[...] = x_f[...] + d2
    out_r[...] = r - apply(d2, 4, level_f) * mask

    halo_sent(bufs_f, rbuf_f.shape[0], 4)
    halo_sent(bufs_m, rbuf_m.shape[0], 4)
    halo_sent(bufs_r, rbuf_r.shape[0], 2)
    for j in range(1, npy):
        sum_copy("py", j).wait_send()
    for j in range(1, npx):
        sum_copy("px", j).wait_send()


def body(
    right_side,
    live_blocks,
    diag_fine,
    couple_fine,
    links_fine,
    send_fine,
    prolong_fine,
    owner_fine,
    diag_mid,
    couple_mid,
    links_mid,
    send_mid,
    prolong_mid,
    owner_mid,
    diag_row,
    couple_row,
    links_row,
    send_row,
    prolong_row,
    owner_row,
    coarse_inverse,
    cheb_low,
    cheb_high,
):
    npx, npy = lax.axis_size("px"), lax.axis_size("py")
    fine, sides, node = right_side.shape[2:]
    mid = diag_mid.shape[2]
    row = diag_row.shape[1]
    k = couple_fine.shape[3]
    size = coarse_inverse.shape[0]
    top = size // node
    h0, h1, h2 = send_fine.shape[-1], send_mid.shape[-1], send_row.shape[-1]
    coarse_most = max(mid, row, top)
    ext_most = max(mid + 4 * h1, row + 2 * h2)

    scalars = (
        live_blocks,
        links_fine.reshape(fine, k),
        send_fine.reshape(1, h0),
        owner_fine.reshape(1, fine),
        links_mid.reshape(mid, k),
        send_mid.reshape(1, h1),
        owner_mid.reshape(1, mid),
        links_row.reshape(row, k),
        send_row,
        owner_row,
        cheb_low,
        cheb_high,
    )
    arrays = (
        diag_fine.reshape(fine, node, node),
        couple_fine.reshape(fine, k * node, node),
        prolong_fine.reshape(fine, node, node),
        diag_mid.reshape(mid, node, node),
        couple_mid.reshape(mid, k * node, node),
        prolong_mid.reshape(mid, node, node),
        diag_row.reshape(row, node, node),
        couple_row.reshape(row, k * node, node),
        prolong_row.reshape(row, node, node),
        coarse_inverse,
    )
    vm = pltpu.VMEM
    dma = pltpu.SemaphoreType.DMA
    scratch = [vm(a.shape, F32) for a in arrays]
    for count in (fine, mid, row):
        scratch += [
            vm((count, node, 2 * node), BF16),
            vm((count, k * node, 2 * node), BF16),
            vm((count, 2 * node, node), BF16),
        ]
    scratch.append(vm((size, 2 * size), BF16))
    scratch += [
        vm((fine, sides, node), F32),
        vm((fine + 4 * h0, 2 * sides, node), BF16),
        vm((fine, sides, node), F32),
        vm((coarse_most, sides, node), F32),
        vm((ext_most, 2 * sides, node), BF16),
        vm((coarse_most, sides, node), F32),
        vm((fine, 2 * sides, node), BF16),
        vm((coarse_most, 2 * sides, node), BF16),
    ]
    for count in (fine, mid, row):
        scratch += [vm((count, sides, node), F32)] * 2
    for uses, dirs, shared in ((5, 4, h0), (4, 4, h1), (4, 2, h2)):
        scratch += [
            vm((uses, shared, sides, node), F32),
            vm((uses, dirs, shared, sides, node), F32),
        ]
    scratch += [
        vm((row, sides, node), F32),
        vm((npy - 1, row, sides, node), F32),
        vm((top, sides, node), F32),
        vm((npx - 1, top, sides, node), F32),
        dma((fine,)),
        dma((9,)),
    ]
    for uses, dirs in ((5, 4), (4, 4), (4, 2)):
        scratch += [dma((uses, dirs))] * 2
    scratch += [dma((npy - 1,))] * 2 + [dma((npx - 1,))] * 2

    shape = jax.ShapeDtypeStruct((fine, sides, node), F32)
    products = fine * (k + 1) * 5 + (mid + row) * (k + 1) * 4 + 2 * (fine + mid + row) + 16
    sol, res = pl.pallas_call(
        functools.partial(kernel, npx, npy),
        out_shape=(shape, shape),
        in_specs=[pl.BlockSpec(memory_space=pltpu.SMEM)] * len(scalars)
        + [pl.BlockSpec(memory_space=pltpu.VMEM)]
        + [pl.BlockSpec(memory_space=pl.ANY)] * len(arrays),
        out_specs=(pl.BlockSpec(memory_space=pltpu.VMEM),) * 2,
        scratch_shapes=scratch,
        compiler_params=pltpu.CompilerParams(
            collective_id=0, has_side_effects=True, vmem_limit_bytes=48 * 1024 * 1024
        ),
        cost_estimate=pl.CostEstimate(
            flops=products * 2 * sides * node * node * 4,
            bytes_accessed=sum(4 * a.size for a in arrays),
            transcendentals=0,
        ),
        name="vcycle",
    )(*scalars, right_side.reshape(fine, sides, node), *arrays)
    full = (1, 1, fine, sides, node)
    return sol.reshape(full), res.reshape(full)


def solution(mesh):
    grid = P("px", "py")
    line = P("px")
    whole = P()
    return jax.shard_map(
        body,
        mesh=mesh,
        in_specs=(grid,) * 14 + (line,) * 6 + (whole,) * 3,
        out_specs=(grid, grid),
        check_vma=False,
    )
```

time: 336 us -> 77 us (0.23)
  the two profiles are of different devices: /device:TPU:18 before, /device:TPU:1 now
where the time goes in v1:
time: 77 us; the launch traced here: 76.4 us
  Pallas kernels  56.9 us (74%)
  local copies, waits for them, and re-layouts  16.8 us (22%)
  between operations  2.6 us (3%)
    pallas_call x1, Pallas kernels, body(): pl.pallas_call(functools.partial(kernel, npx, npy), out_shape=(shape, sha...  56.9 us
    unnamed x36, local copies, waits for them, and re-layouts  16.1 us

profile of v1, /device:TPU:1, one launch (start us, length us, event | category | flops | bytes accessed | tf_op | source)
XLA Modules:
  0.0 76.4 jit_solution(1537122083174865199)
XLA Ops:
  2.6 0.8 copy.25.links_fine
  3.3 0.0 copy-start
  3.3 1.2 %copy-done = f32[1,1,16,128,128]{4,3,2,1,0:T(8,128)S(1)} copy-done((f32[1,1,16,128,128]{4,3,2,1,0:T(8,128)S(1)}, f32[1,1,16,128,128]{4,3,2,1,0:T(8,128)}, u32[]{:S(2)}) %copy-start) | copy-done | bytes 1048600
  4.6 0.0 copy-start.1
  4.6 1.2 %copy-done.1 = f32[1,1,16,128,128]{4,3,2,1,0:T(8,128)S(1)} copy-done((f32[1,1,16,128,128]{4,3,2,1,0:T(8,128)S(1)}, f32[1,1,16,128,128]{4,3,2,1,0:T(8,128)}, u32[]{:S(2)}) %copy-start.1) | copy-done | bytes 1048600
  5.8 0.0 copy-start.2
  5.8 1.2 %copy-done.2 = f32[1,1,4,4,128,128]{5,4,3,2,1,0:T(8,128)S(1)} copy-done((f32[1,1,4,4,128,128]{5,4,3,2,1,0:T(8,128)S(1)}, f32[1,1,4,4,128,128]{5,4,3,2,1,0:T(8,128)}, u32[]{:S(2)}) %copy-start.2) | copy-done | bytes 1048600
  7.0 0.0 copy-start.3
  7.0 1.2 %copy-done.3 = f32[1,4,4,128,128]{4,3,2,1,0:T(8,128)S(1)} copy-done((f32[1,4,4,128,128]{4,3,2,1,0:T(8,128)S(1)}, f32[1,4,4,128,128]{4,3,2,1,0:T(8,128)}, u32[]{:S(2)}) %copy-start.3) | copy-done | bytes 1048600
  8.2 0.0 copy-start.4
  8.2 0.9 %copy-done.4 = f32[1,1,4,128,128]{4,3,2,1,0:T(8,128)S(1)} copy-done((f32[1,1,4,128,128]{4,3,2,1,0:T(8,128)S(1)}, f32[1,1,4,128,128]{4,3,2,1,0:T(8,128)}, u32[]{:S(2)}) %copy-start.4) | copy-done | bytes 262168
  9.2 0.0 copy-start.5
  9.2 0.9 %copy-done.5 = f32[1,1,4,128,128]{4,3,2,1,0:T(8,128)S(1)} copy-done((f32[1,1,4,128,128]{4,3,2,1,0:T(8,128)S(1)}, f32[1,1,4,128,128]{4,3,2,1,0:T(8,128)}, u32[]{:S(2)}) %copy-start.5) | copy-done | bytes 262168
  10.1 0.0 copy-start.6
  10.1 0.9 %copy-done.6 = f32[1,4,128,128]{3,2,1,0:T(8,128)S(1)} copy-done((f32[1,4,128,128]{3,2,1,0:T(8,128)S(1)}, f32[1,4,128,128]{3,2,1,0:T(8,128)}, u32[]{:S(2)}) %copy-start.6) | copy-done | bytes 262168
  11.1 0.0 copy-start.7
  11.1 0.9 %copy-done.7 = f32[1,4,128,128]{3,2,1,0:T(8,128)S(1)} copy-done((f32[1,4,128,128]{3,2,1,0:T(8,128)S(1)}, f32[1,4,128,128]{3,2,1,0:T(8,128)}, u32[]{:S(2)}) %copy-start.7) | copy-done | bytes 262168
  12.0 0.0 copy-start.8
  12.0 0.8 %copy-done.8 = f32[1,1,16,8,128]{4,3,2,1,0:T(8,128)S(1)} copy-done((f32[1,1,16,8,128]{4,3,2,1,0:T(8,128)S(1)}, f32[1,1,16,8,128]{4,3,2,1,0:T(8,128)}, u32[]{:S(2)}) %copy-start.8) | copy-done | bytes 65560
  12.9 0.0 copy-start.9
  12.9 0.7 copy-done.9
  13.6 0.0 copy-start.10
  13.6 0.7 copy-done.10
  14.2 0.0 copy-start.11
  14.2 0.7 copy-done.11
  14.9 0.0 copy-start.12
  14.9 0.7 copy-done.12
  15.5 0.0 copy-start.13
  15.5 0.7 copy-done.13
  16.2 0.0 copy-start.14
  16.2 0.7 copy-done.14
  16.9 0.0 copy-start.15
  16.9 0.7 copy-done.15
  17.5 0.0 copy-start.16
  17.5 0.7 copy-done.16
  18.2 56.9 %vcycle.1 = (f32[16,8,128]{2,1,0:T(8,128)S(1)}, f32[16,8,128]{2,1,0:T(8,128)S(1)}) custom-call(s32[1,1]{1,0:T(1,128)S(6)} %copy.28.live, s32[16,4]{1,0:T(8,128)S(1)} %copy.25.links_fine, s32[1,4]{1,0:T(1,128)S(1)} %bitcast.33, s32[1,16]{1,0:T(1,128)S(1)} %bitcast.34, s32[4,4]{1,0:T(4,128)S(1)} %bitcast.31, s32[1,1]{1,0:T(1,128)} %bitcast.19.send_mid, ...), custom_call_target="tpu_custom_call" | custom-call | flops 654311424 | bytes 10485760 | tf_op jit(solution)/shard_map/vcycle/pallas_call | solution.py:538
  75.1 0.6 copy.31
  75.8 0.6 copy.32
Async XLA Ops:
  3.3 1.2 %copy-start = (f32[1,1,16,128,128]{4,3,2,1,0:T(8,128)S(1)}, f32[1,1,16,128,128]{4,3,2,1,0:T(8,128)}, u32[]{:S(2)}) copy-start(f32[1,1,16,128,128]{4,3,2,1,0:T(8,128)} %param.25) | copy-start | bytes 3145732
  4.6 1.2 %copy-start.1 = (f32[1,1,16,128,128]{4,3,2,1,0:T(8,128)S(1)}, f32[1,1,16,128,128]{4,3,2,1,0:T(8,128)}, u32[]{:S(2)}) copy-start(f32[1,1,16,128,128]{4,3,2,1,0:T(8,128)} %param.29) | copy-start | bytes 3145732
  5.8 1.2 %copy-start.2 = (f32[1,1,4,4,128,128]{5,4,3,2,1,0:T(8,128)S(1)}, f32[1,1,4,4,128,128]{5,4,3,2,1,0:T(8,128)}, u32[]{:S(2)}) copy-start(f32[1,1,4,4,128,128]{5,4,3,2,1,0:T(8,128)} %param.32) | copy-start | bytes 3145732
  7.0 1.2 %copy-start.3 = (f32[1,4,4,128,128]{4,3,2,1,0:T(8,128)S(1)}, f32[1,4,4,128,128]{4,3,2,1,0:T(8,128)}, u32[]{:S(2)}) copy-start(f32[1,4,4,128,128]{4,3,2,1,0:T(8,128)} %param.38) | copy-start | bytes 3145732
  8.2 0.9 %copy-start.4 = (f32[1,1,4,128,128]{4,3,2,1,0:T(8,128)S(1)}, f32[1,1,4,128,128]{4,3,2,1,0:T(8,128)}, u32[]{:S(2)}) copy-start(f32[1,1,4,128,128]{4,3,2,1,0:T(8,128)} %param.31) | copy-start | bytes 786436
  9.2 0.9 %copy-start.5 = (f32[1,1,4,128,128]{4,3,2,1,0:T(8,128)S(1)}, f32[1,1,4,128,128]{4,3,2,1,0:T(8,128)}, u32[]{:S(2)}) copy-start(f32[1,1,4,128,128]{4,3,2,1,0:T(8,128)} %param.35) | copy-start | bytes 786436
  10.1 0.9 %copy-start.6 = (f32[1,4,128,128]{3,2,1,0:T(8,128)S(1)}, f32[1,4,128,128]{3,2,1,0:T(8,128)}, u32[]{:S(2)}) copy-start(f32[1,4,128,128]{3,2,1,0:T(8,128)} %param.37) | copy-start | bytes 786436
  11.1 0.9 %copy-start.7 = (f32[1,4,128,128]{3,2,1,0:T(8,128)S(1)}, f32[1,4,128,128]{3,2,1,0:T(8,128)}, u32[]{:S(2)}) copy-start(f32[1,4,128,128]{3,2,1,0:T(8,128)} %param.41) | copy-start | bytes 786436
  12.0 0.8 %copy-start.8 = (f32[1,1,16,8,128]{4,3,2,1,0:T(8,128)S(1)}, f32[1,1,16,8,128]{4,3,2,1,0:T(8,128)}, u32[]{:S(2)}) copy-start(f32[1,1,16,8,128]{4,3,2,1,0:T(8,128)} %param.23) | copy-start | bytes 196612
  12.9 0.7 copy-start.9
  13.6 0.7 copy-start.10
  14.2 0.7 copy-start.11
  14.9 0.7 copy-start.12
  15.5 0.7 copy-start.13
  16.2 0.7 copy-start.14
  16.9 0.7 copy-start.15
  17.5 0.7 copy-start.16

commit v2 on v1

--- a/solution.py
+++ b/solution.py
@@ -31,19 +31,26 @@
 def kernel(
     npx,
     npy,
-    live,
-    links_fine,
-    send_fine,
-    owner_fine,
-    links_mid,
-    send_mid,
-    owner_mid,
-    links_row,
-    send_row,
-    owner_row,
-    cheb_low,
-    cheb_high,
-    right_side,
+    *refs,
+):
+    scalars_hbm, refs = refs[:12], refs[12:]
+    scalars, refs = refs[-13:-1], refs[:-13] + refs[-1:]
+    (
+        live,
+        links_fine,
+        send_fine,
+        owner_fine,
+        links_mid,
+        send_mid,
+        owner_mid,
+        links_row,
+        send_row,
+        owner_row,
+        cheb_low,
+        cheb_high,
+    ) = scalars
+    (
+    right_hbm,
     diag_fine,
     couple_fine,
     prolong_fine,
@@ -54,8 +61,7 @@
     couple_row,
     prolong_row,
     inverse,
-    out_x,
-    out_r,
+    out,
     stage_df,
     stage_cf,
     stage_pf,
@@ -112,7 +118,9 @@
     rs_y,
     ss_x,
     rs_x,
-):
+    right_side,
+    load_s,
+    ) = refs
     px = lax.axis_index("px")
     py = lax.axis_index("py")
     fine = diag_fine.shape[0]
@@ -120,10 +128,24 @@
     row = diag_row.shape[0]
     node = diag_fine.shape[-1]
     top = inverse.shape[0] // node
-    width_k = links_fine.shape[1]
-
-    def couple_copy(b):
-        return pltpu.make_async_copy(couple_fine.at[b], stage_cf.at[b], load_cf.at[b])
+    width_k = links_mid.shape[1]
+
+    barrier = pltpu.get_barrier_semaphore()
+    for j in range(1, npx):
+        pl.semaphore_signal(
+            barrier, inc=1, device_id={"px": lax.rem(px + j, npx)}, device_id_type=MESH
+        )
+    for j in range(1, npy):
+        pl.semaphore_signal(
+            barrier, inc=1, device_id={"py": lax.rem(py + j, npy)}, device_id_type=MESH
+        )
+
+    parts = load_cf.shape[0]
+    per_part = fine // parts
+
+    def couple_copy(i):
+        blocks = pl.ds(i * per_part, per_part)
+        return pltpu.make_async_copy(couple_fine.at[blocks], stage_cf.at[blocks], load_cf.at[i])
 
     def whole_copy(i):
         src, dst = (
@@ -139,24 +161,21 @@
         )[i]
         return pltpu.make_async_copy(src, dst, load.at[i])
 
+    small = [
+        pltpu.make_async_copy(src, dst, load_s.at[i])
+        for i, (src, dst) in enumerate(
+            zip(scalars_hbm + (right_hbm,), scalars + (right_side,))
+        )
+    ]
+    for copy in small:
+        copy.start()
     whole_copy(0).start()
 
-    @pl.loop(0, fine)
-    def _(b):
-        couple_copy(b).start()
+    for i in range(parts):
+        couple_copy(i).start()
 
     for i in range(1, 9):
         whole_copy(i).start()
-
-    barrier = pltpu.get_barrier_semaphore()
-    for j in range(1, npx):
-        pl.semaphore_signal(
-            barrier, inc=1, device_id={"px": lax.rem(px + j, npx)}, device_id_type=MESH
-        )
-    for j in range(1, npy):
-        pl.semaphore_signal(
-            barrier, inc=1, device_id={"py": lax.rem(py + j, npy)}, device_id_type=MESH
-        )
 
     has = (px > 0, px < npx - 1, py > 0, py < npy - 1)
     for d in range(4):
@@ -182,7 +201,7 @@
         )
 
     def halo_start(bufs, e, dirs):
-        for d in range(dirs):
+        for d in reversed(range(dirs)):
 
             @pl.when(has[d ^ 1])
             def _(d=d):
@@ -247,10 +266,12 @@
             how(stage, w, b)
 
     def split_couple_fine():
-        @pl.loop(0, fine)
-        def _(b):
-            couple_copy(b).wait()
-            split_cols(stage_cf, w_cf, b)
+        for i in range(parts):
+            couple_copy(i).wait()
+
+            @pl.loop(i * per_part, (i + 1) * per_part)
+            def _(b):
+                split_cols(stage_cf, w_cf, b)
 
     def split_inverse():
         whole_copy(8).wait()
@@ -286,7 +307,7 @@
             ext[count + d * shared : count + (d + 1) * shared] = rows_split(bufs[1][e, d])
 
         def far(b, carry):
-            picked = jnp.concatenate([ext[links[b, k]] for k in range(width_k)], axis=1)
+            picked = jnp.concatenate([ext[links(b, k)] for k in range(width_k)], axis=1)
             acc[b] += quarters(jnp.dot(picked, w_c[b], preferred_element_type=F32))
             return carry
 
@@ -318,7 +339,7 @@
         return jnp.stack(out)
 
     def terms(level):
-        shape = right_side.shape[1:]
+        shape = out.shape[2:]
         low = jnp.full(shape, cheb_low[level], F32)
         high = jnp.full(shape, cheb_high[level], F32)
         center = 0.5 * (high + low)
@@ -331,10 +352,12 @@
     bufs_f = (sbuf_f, rbuf_f, ss_f, rs_f)
     bufs_m = (sbuf_m, rbuf_m, ss_m, rs_m)
     bufs_r = (sbuf_r, rbuf_r, ss_r, rs_r)
-    level_f = (fine, vec_f, ext_f, acc_f, bufs_f, 4, links_fine, send_fine, w_df, w_cf)
-    level_m = (mid, vec_c, ext_c, acc_c, bufs_m, 4, links_mid, send_mid, w_dm, w_cm)
-    level_r = (row, vec_c, ext_c, acc_c, bufs_r, 2, links_row, send_row, w_dr, w_cr)
-
+    level_f = (fine, vec_f, ext_f, acc_f, bufs_f, 4, lambda b, k: links_fine[k, b], send_fine, w_df, w_cf)
+    level_m = (mid, vec_c, ext_c, acc_c, bufs_m, 4, lambda b, k: links_mid[b, k], send_mid, w_dm, w_cm)
+    level_r = (row, vec_c, ext_c, acc_c, bufs_r, 2, lambda b, k: links_row[b, k], send_row, w_dr, w_cr)
+
+    for copy in small:
+        copy.wait()
     mask = jnp.where(
         lax.broadcasted_iota(jnp.int32, right_side.shape, 0) < live[0, 0], 1.0, 0.0
     ).astype(F32)
@@ -420,8 +443,8 @@
     x_f[...] += d
     r = r - apply(d, 3, level_f) * mask
     d2 = carry_c * d + gain_c * r
-    out_x[...] = x_f[...] + d2
-    out_r[...] = r - apply(d2, 4, level_f) * mask
+    out[0] = x_f[...] + d2
+    out[1] = r - apply(d2, 4, level_f) * mask
 
     halo_sent(bufs_f, rbuf_f.shape[0], 4)
     halo_sent(bufs_m, rbuf_m.shape[0], 4)
@@ -470,7 +493,7 @@
 
     scalars = (
         live_blocks,
-        links_fine.reshape(fine, k),
+        jnp.swapaxes(links_fine.reshape(fine, k), 0, 1),
         send_fine.reshape(1, h0),
         owner_fine.reshape(1, fine),
         links_mid.reshape(mid, k),
@@ -526,25 +549,26 @@
         vm((npy - 1, row, sides, node), F32),
         vm((top, sides, node), F32),
         vm((npx - 1, top, sides, node), F32),
-        dma((fine,)),
+        dma((4 if fine % 4 == 0 else 1,)),
         dma((9,)),
     ]
     for uses, dirs in ((5, 4), (4, 4), (4, 2)):
         scratch += [dma((uses, dirs))] * 2
     scratch += [dma((npy - 1,))] * 2 + [dma((npx - 1,))] * 2
-
-    shape = jax.ShapeDtypeStruct((fine, sides, node), F32)
+    scratch.append(vm((fine, sides, node), F32))
+    scratch += [pltpu.SMEM(a.shape, a.dtype) for a in scalars]
+    scratch.append(dma((len(scalars) + 1,)))
+
+    shape = jax.ShapeDtypeStruct((2, fine, sides, node), F32)
     products = fine * (k + 1) * 5 + (mid + row) * (k + 1) * 4 + 2 * (fine + mid + row) + 16
-    sol, res = pl.pallas_call(
+    out = pl.pallas_call(
         functools.partial(kernel, npx, npy),
-        out_shape=(shape, shape),
-        in_specs=[pl.BlockSpec(memory_space=pltpu.SMEM)] * len(scalars)
-        + [pl.BlockSpec(memory_space=pltpu.VMEM)]
-        + [pl.BlockSpec(memory_space=pl.ANY)] * len(arrays),
-        out_specs=(pl.BlockSpec(memory_space=pltpu.VMEM),) * 2,
+        out_shape=shape,
+        in_specs=[pl.BlockSpec(memory_space=pltpu.HBM)] * (len(scalars) + 1 + len(arrays)),
+        out_specs=pl.BlockSpec(memory_space=pltpu.VMEM),
         scratch_shapes=scratch,
         compiler_params=pltpu.CompilerParams(
-            collective_id=0, has_side_effects=True, vmem_limit_bytes=48 * 1024 * 1024
+            collective_id=0, has_side_effects=True, vmem_limit_bytes=56 * 1024 * 1024
         ),
         cost_estimate=pl.CostEstimate(
             flops=products * 2 * sides * node * node * 4,
@@ -554,7 +578,7 @@
         name="vcycle",
     )(*scalars, right_side.reshape(fine, sides, node), *arrays)
     full = (1, 1, fine, sides, node)
-    return sol.reshape(full), res.reshape(full)
+    return out[0].reshape(full), out[1].reshape(full)
 
 
 def solution(mesh):

time: 77 us -> 61.4 us (0.80)
  local copies, waits for them, and re-layouts: 16.8 us -> 1.53 us
    unnamed x36 -> x0, local copies, waits for them, and re-layouts: 16.1 us -> none
    another operation x0 -> x1, local copies, waits for them, and re-layouts: none -> 1.53 us  [body(): return (out[0].reshape(full), out[1].reshape(full))]
where the time goes in v2:
time: 61.4 us; the launch traced here: 61.2 us
  Pallas kernels  57.1 us (93%)
  between operations  2.58 us (4%)
  local copies, waits for them, and re-layouts  1.53 us (2%)
    pallas_call x1, Pallas kernels, body(): pl.pallas_call(functools.partial(kernel, npx, npy), out_shape=shape, in_s...  57.1 us
    another operation x1, local copies, waits for them, and re-layouts, body(): return (out[0].reshape(full), out[1].reshape(full))  1.53 us

profile of v2, /device:TPU:1, one launch (start us, length us, event | category | flops | bytes accessed | tf_op | source)
XLA Modules:
  0.0 61.2 jit_solution(5854836364961351505)
XLA Ops:
  2.6 57.1 %vcycle.1 = f32[2,16,8,128]{3,2,1,0:T(8,128)} custom-call(s32[1,1]{1,0:T(1,128)S(6)} %copy.25.refs_0_, s32[4,16]{1,0:T(4,128)} %bitcast.34, s32[1,4]{1,0:T(1,128)} %bitcast.37, s32[1,16]{1,0:T(1,128)} %bitcast.38, s32[4,4]{1,0:T(4,128)} %bitcast.35, s32[1,1]{1,0:T(1,128)} %bitcast.23.refs_5_, s32[1,4]{1,0:T(1,128)} %bitcast.39, s32[4,4]{1,0:T(4,128)} %bitcast.36, ...), custom_call_target="tpu_custom_call" | custom-call | flops 654311424 | bytes 10485760 | tf_op jit(solution)/shard_map/vcycle/pallas_call | solution.py:564
  59.7 1.5 %slice_bitcast_fusion = (f32[1,1,16,8,128]{4,3,2,1,0:T(8,128)}, f32[1,1,16,8,128]{4,3,2,1,0:T(8,128)}) fusion(f32[2,16,8,128]{3,2,1,0:T(8,128)} %vcycle.1), kind=kLoop, calls=%fused_computation | loop fusion | bytes 262144 | tf_op jit(solution)/shard_map/reshape;squeeze | solution.py:581

commit v3 on v2

--- a/solution.py
+++ b/solution.py
@@ -214,8 +214,8 @@
             def _(d=d):
                 halo_copy(bufs, e, d, d).wait_recv()
 
-    def halo_sent(bufs, count, dirs):
-        for e in range(count):
+    def halo_sent(bufs, uses, dirs):
+        for e in uses:
             for d in range(dirs):
 
                 @pl.when(has[d ^ 1])
@@ -284,13 +284,14 @@
             w_inv[rows, :size] = high.astype(BF16)
             w_inv[rows, size:] = low.astype(BF16)
 
-    def apply(v, e, level, before_diag=None, before_couple=None):
+    def apply(v, e, level, before_diag=None, before_couple=None, sent=False, following=None):
         count, vec, ext, acc, bufs, dirs, links, send, w_d, w_c = level
         shared = send.shape[1]
-        vec[:count] = v
-        for h in range(shared):
-            bufs[0][e, h] = vec[send[0, h]]
-        halo_start(bufs, e, dirs)
+        if not sent:
+            vec[:count] = v
+            for h in range(shared):
+                bufs[0][e, h] = vec[send[0, h]]
+            halo_start(bufs, e, dirs)
         ext[:count] = rows_split(v)
         if before_diag is not None:
             before_diag()
@@ -306,9 +307,23 @@
         for d in range(dirs):
             ext[count + d * shared : count + (d + 1) * shared] = rows_split(bufs[1][e, d])
 
+        def product(b):
+            picked = jnp.concatenate([ext[links(b, k)] for k in range(width_k)], axis=1)
+            return acc[b] + quarters(jnp.dot(picked, w_c[b], preferred_element_type=F32))
+
+        if following is not None:
+            p, q, keep = following
+            vec[:count] = p
+            for h in range(shared):
+                b = send[0, h]
+                z = product(b)
+                if keep is not None:
+                    z = z * keep(b)
+                bufs[0][e + 1, h] = vec[b] - q[0] * z
+            halo_start(bufs, e + 1, dirs)
+
         def far(b, carry):
-            picked = jnp.concatenate([ext[links(b, k)] for k in range(width_k)], axis=1)
-            acc[b] += quarters(jnp.dot(picked, w_c[b], preferred_element_type=F32))
+            acc[b] = product(b)
             return carry
 
         lax.fori_loop(0, count, far, 0, unroll=True)
@@ -362,6 +377,9 @@
         lax.broadcasted_iota(jnp.int32, right_side.shape, 0) < live[0, 0], 1.0, 0.0
     ).astype(F32)
 
+    def is_live(b):
+        return jnp.where(b < live[0, 0], 1.0, 0.0)
+
     inv_c, carry_c, gain_c = terms(0)
     target = right_side[...] * mask
     b_f[...] = target
@@ -373,6 +391,7 @@
         level_f,
         before_diag=lambda: split_all(0, stage_df, w_df, split_cols),
         before_couple=split_couple_fine,
+        following=(carry_c * d + gain_c * target, gain_c, is_live),
     )
     r = target - ad * mask
     d2 = carry_c * d + gain_c * r
@@ -383,14 +402,18 @@
         split_all(2, stage_dm, w_dm, split_cols)
         split_all(3, stage_cm, w_cm, split_cols)
 
-    r = r - apply(d2, 1, level_f, before_couple=more) * mask
+    r = r - apply(d2, 1, level_f, before_couple=more, sent=True) * mask
 
     inv_c, carry_c, gain_c = terms(1)
     target = restrict(r, w_pf, owner_fine, fine, mid, split_f)
     b_m[...] = target
     d = target * inv_c
     r = target - apply(
-        d, 0, level_m, before_couple=lambda: split_all(4, stage_pm, w_pm, split_rows)
+        d,
+        0,
+        level_m,
+        before_couple=lambda: split_all(4, stage_pm, w_pm, split_rows),
+        following=(carry_c * d + gain_c * target, gain_c, None),
     )
     d2 = carry_c * d + gain_c * r
     x_m[...] = d + d2
@@ -400,17 +423,23 @@
         split_all(6, stage_cr, w_cr, split_cols)
         split_all(7, stage_pr, w_pr, split_rows)
 
-    r = r - apply(d2, 1, level_m, before_couple=row_split)
+    r = r - apply(d2, 1, level_m, before_couple=row_split, sent=True)
 
     inv_c, carry_c, gain_c = terms(2)
     share = restrict(r, w_pm, owner_mid, mid, row, split_c)
     target = all_sum("py", npy, sum_y_src, sum_y, share)
     b_r[...] = target
     d = target * inv_c
-    r = target - apply(d, 0, level_r, before_couple=split_inverse)
+    r = target - apply(
+        d,
+        0,
+        level_r,
+        before_couple=split_inverse,
+        following=(carry_c * d + gain_c * target, gain_c, None),
+    )
     d2 = carry_c * d + gain_c * r
     x_r[...] = d + d2
-    r = r - apply(d2, 1, level_r)
+    r = r - apply(d2, 1, level_r, sent=True)
 
     part = restrict(r, w_pr, owner_row, row, top, split_c)
     top_target = all_sum("px", npx, sum_x_src, sum_x, part)
@@ -420,39 +449,54 @@
 
     x = x_r[...] + prolong(top_sol, w_pr, owner_row, row, split_c)
     x_r[...] = x
-    r = b_r[...] - apply(x, 2, level_r)
+    r = b_r[...] - apply(x, 2, level_r, following=(inv_c * b_r[...], inv_c, None))
     d = r * inv_c
     x_r[...] += d
-    r = r - apply(d, 3, level_r)
+    r = r - apply(d, 3, level_r, sent=True)
     x = x_r[...] + carry_c * d + gain_c * r
 
     inv_c, carry_c, gain_c = terms(1)
     x = x_m[...] + prolong(x, w_pm, owner_mid, mid, split_c)
     x_m[...] = x
-    r = b_m[...] - apply(x, 2, level_m)
+    r = b_m[...] - apply(x, 2, level_m, following=(inv_c * b_m[...], inv_c, None))
     d = r * inv_c
     x_m[...] += d
-    r = r - apply(d, 3, level_m)
+    r = r - apply(d, 3, level_m, sent=True)
     x = x_m[...] + carry_c * d + gain_c * r
+
+    def coarse_sent():
+        halo_sent(bufs_m, range(4), 4)
+        halo_sent(bufs_r, range(4), 2)
+        for j in range(1, npy):
+            sum_copy("py", j).wait_send()
+        for j in range(1, npx):
+            sum_copy("px", j).wait_send()
 
     inv_c, carry_c, gain_c = terms(0)
     x = x_f[...] + prolong(x, w_pf, owner_fine, fine, split_c) * mask
     x_f[...] = x
-    r = b_f[...] - apply(x, 2, level_f) * mask
+    r = b_f[...] - apply(
+        x, 2, level_f, before_couple=coarse_sent, following=(inv_c * b_f[...], inv_c, is_live)
+    ) * mask
     d = r * inv_c
     x_f[...] += d
-    r = r - apply(d, 3, level_f) * mask
+    r = (
+        r
+        - apply(
+            d,
+            3,
+            level_f,
+            before_couple=lambda: halo_sent(bufs_f, range(3), 4),
+            sent=True,
+            following=(carry_c * d + gain_c * r, gain_c, is_live),
+        )
+        * mask
+    )
     d2 = carry_c * d + gain_c * r
     out[0] = x_f[...] + d2
-    out[1] = r - apply(d2, 4, level_f) * mask
-
-    halo_sent(bufs_f, rbuf_f.shape[0], 4)
-    halo_sent(bufs_m, rbuf_m.shape[0], 4)
-    halo_sent(bufs_r, rbuf_r.shape[0], 2)
-    for j in range(1, npy):
-        sum_copy("py", j).wait_send()
-    for j in range(1, npx):
-        sum_copy("px", j).wait_send()
+    out[1] = r - apply(d2, 4, level_f, sent=True) * mask
+
+    halo_sent(bufs_f, (3, 4), 4)
 
 
 def body(

time: 61.4 us -> 59.9 us (0.976)
  Pallas kernels: 57.1 us -> 55.6 us
    pallas_call x1, Pallas kernels: 57.1 us -> 55.6 us  [body(): pl.pallas_call(functools.partial(kernel, npx, npy), out_shape=shape, in_s...]
where the time goes in v3:
time: 59.9 us; the launch traced here: 59.7 us
  Pallas kernels  55.6 us (93%)
  between operations  2.58 us (4%)
  local copies, waits for them, and re-layouts  1.53 us (3%)
    pallas_call x1, Pallas kernels, body(): pl.pallas_call(functools.partial(kernel, npx, npy), out_shape=shape, in_s...  55.6 us
    another operation x1, local copies, waits for them, and re-layouts, body(): return (out[0].reshape(full), out[1].reshape(full))  1.53 us

profile of v3, /device:TPU:1, one launch (start us, length us, event | category | flops | bytes accessed | tf_op | source)
XLA Modules:
  0.0 59.7 jit_solution(6012170944346386410)
XLA Ops:
  2.6 55.6 %vcycle.1 = f32[2,16,8,128]{3,2,1,0:T(8,128)} custom-call(s32[1,1]{1,0:T(1,128)S(6)} %copy.25.refs_0_, s32[4,16]{1,0:T(4,128)} %bitcast.34, s32[1,4]{1,0:T(1,128)} %bitcast.37, s32[1,16]{1,0:T(1,128)} %bitcast.38, s32[4,4]{1,0:T(4,128)} %bitcast.35, s32[1,1]{1,0:T(1,128)} %bitcast.23.refs_5_, s32[1,4]{1,0:T(1,128)} %bitcast.39, s32[4,4]{1,0:T(4,128)} %bitcast.36, ...), custom_call_target="tpu_custom_call" | custom-call | flops 654311424 | bytes 10485760 | tf_op jit(solution)/shard_map/vcycle/pallas_call | solution.py:608
  58.1 1.5 %slice_bitcast_fusion = (f32[1,1,16,8,128]{4,3,2,1,0:T(8,128)}, f32[1,1,16,8,128]{4,3,2,1,0:T(8,128)}) fusion(f32[2,16,8,128]{3,2,1,0:T(8,128)} %vcycle.1), kind=kLoop, calls=%fused_computation | loop fusion | bytes 262144 | tf_op jit(solution)/shard_map/reshape;squeeze | solution.py:625
